TPU v7x, 32 devices: a whole 2x2x4 slice. The times are simulated.
32 devices in a mesh: train: 4 (over y, x), roll: 8 (over z, core).
Axes of the slice: x: 2, y: 2, z: 4, core: 2. Of those that a mesh axis runs over, the one named last changes fastest.
Arguments:
- master_gate: float32 [4, 2048, 7168], P(None, 'roll', 'train'), may hold values from -1 to 1
- master_up: float32 [4, 2048, 7168], P(None, 'roll', 'train'), may hold values from -1 to 1
- master_down: float32 [4, 2048, 7168], P(None, 'roll', 'train'), may hold values from -1 to 1
- tokens: bfloat16 [512, 7168], P('roll'), may hold values from -6 to 6
- expert_ids: int32 [512, 2], P('roll'), may hold values from 0 to 3, all different within a row; in each aligned block of 64 rows (0 to 63, 64 to 127, ...) at most 32 rows name the same one
- gate_weights: float32 [512, 2], P('roll'), may hold values from 0.2 to 1
- placement: int32 [8], replicated, may hold values from 0 to 3, as said below
Outputs:
- slot_gate: bfloat16 [8, 16, 128, 7168], P('roll', None, 'train')
- slot_up: bfloat16 [8, 16, 128, 7168], P('roll', None, 'train')
- slot_down: bfloat16 [8, 16, 128, 7168], P('roll', None, 'train')
- mixed_out: bfloat16 [512, 7168], P('roll', 'train')
Inputs may be any that keep to these rules, and one draw needn't show every extreme that they name: `expert_ids`: the 2 experts of a row differ. In each aligned block of 64 rows (the rows of one index of roll) no expert is named by more than 32 rows, a bound that some block reaches. `placement`: every expert of the window is held by exactly two owners.
All inputs are finite; a program needn't handle non-finite values. Where the computation divides by a largest or mean magnitude, that divisor is 1e-20 or more.
Results may differ from a plain program's by a relative error of at most 0.0093.
Values may be sent and summed in bfloat16 or wider, within the bound.
No kernel may reach another device: no remote copies, remote signals or barrier semaphores. Data moves between devices by JAX's collectives and lax.ppermute only.
A program may use at most 256 MiB of HBM per device.

v0:
```python
import jax
import jax.numpy as jnp
from jax import lax
from jax.sharding import PartitionSpec as P

BLOCK = 128
TOP = 2
CAP = 16


def quantize_local(master):
    experts, hidden_rows, features = master.shape
    blocks = master.reshape(experts, hidden_rows // BLOCK, BLOCK, features // BLOCK, BLOCK)
    block_scale = jnp.max(jnp.abs(blocks), axis=(2, 4)).astype(jnp.bfloat16)
    quantized = (blocks / block_scale.astype(jnp.float32)[:, :, None, :, None]).astype(jnp.bfloat16)
    return (quantized.reshape(experts, hidden_rows // BLOCK, BLOCK, features), block_scale)


def dequantize_slot(quantized, block_scale):
    groups, group_rows, features = quantized.shape
    spread_out = quantized.astype(jnp.float32).reshape(groups, group_rows, features // BLOCK, BLOCK)
    restored = spread_out * block_scale.astype(jnp.float32)[:, :, :, None]
    return restored.astype(jnp.bfloat16).reshape(groups * group_rows, features)


def per_device(master_gate, master_up, master_down, tokens, expert_ids, gate_weights, placement):
    trains = lax.axis_size("train")
    owners = lax.axis_size("roll")
    quant_gate, scale_gate = quantize_local(master_gate)
    quant_up, scale_up = quantize_local(master_up)
    quant_down, scale_down = quantize_local(master_down)
    scales = jnp.stack((scale_gate, scale_up, scale_down), axis=-1)
    experts, local_blocks, block_rows, local_features = quant_gate.shape
    scale_blocks = scales.shape[2]
    all_blocks = owners * local_blocks
    picked_gate = jnp.take(quant_gate, placement, axis=0)
    picked_up = jnp.take(quant_up, placement, axis=0)
    picked_down = jnp.take(quant_down, placement, axis=0)
    picked_scales = jnp.take(scales, placement, axis=0)
    got_gate, got_up, got_down, got_scales = (
        lax.all_to_all(picked_gate, "roll", split_axis=0, concat_axis=0, tiled=True),
        lax.all_to_all(picked_up, "roll", split_axis=0, concat_axis=0, tiled=True),
        lax.all_to_all(picked_down, "roll", split_axis=0, concat_axis=0, tiled=True),
        lax.all_to_all(picked_scales, "roll", split_axis=0, concat_axis=0, tiled=True),
    )
    flat_shape = (all_blocks, block_rows, local_features)
    spread_scales = jnp.broadcast_to(
        got_scales.reshape(all_blocks, 1, scale_blocks, 3), (all_blocks, trains, scale_blocks, 3)
    )
    slot_gate, slot_up, slot_down, slot_scales = (
        lax.all_to_all(
            got_gate.reshape(flat_shape), "train", split_axis=1, concat_axis=2, tiled=True
        ),
        lax.all_to_all(
            got_up.reshape(flat_shape), "train", split_axis=1, concat_axis=2, tiled=True
        ),
        lax.all_to_all(
            got_down.reshape(flat_shape), "train", split_axis=1, concat_axis=2, tiled=True
        ),
        lax.all_to_all(spread_scales, "train", split_axis=1, concat_axis=2, tiled=True),
    )
    dequant_gate = dequantize_slot(slot_gate, slot_scales[..., 0])
    dequant_up = dequantize_slot(slot_up, slot_scales[..., 1])
    dequant_down = dequantize_slot(slot_down, slot_scales[..., 2])
    hidden_units = dequant_gate.shape[0]
    expert_range = jnp.arange(experts, dtype=jnp.int32)
    owner_range = jnp.arange(owners, dtype=jnp.int32)
    holders = (placement[None, :] == expert_range[:, None]).astype(jnp.int32)
    same_expert = (placement[:, None] == placement[None, :]) & (
        owner_range[None, :] < owner_range[:, None]
    )
    copy_rank = jnp.sum(same_expert.astype(jnp.int32), axis=1)
    first_owner = jnp.sum(
        holders * (copy_rank[None, :] == 0).astype(jnp.int32) * owner_range[None, :], axis=1
    )
    second_owner = jnp.sum(
        holders * (copy_rank[None, :] == 1).astype(jnp.int32) * owner_range[None, :], axis=1
    )
    flat_ids = expert_ids.reshape(-1)
    onehot = (flat_ids[:, None] == expert_range[None, :]).astype(jnp.int32)
    before = jnp.cumsum(onehot, axis=0) - onehot
    position = jnp.sum(before * onehot, axis=1)
    row_first = jnp.sum(onehot * first_owner[None, :], axis=1)
    row_second = jnp.sum(onehot * second_owner[None, :], axis=1)
    row_target = jnp.where(position % 2 == 0, row_first, row_second)
    destination = row_target * CAP + position // 2
    slot_count = owners * CAP
    source = (
        jnp.zeros((slot_count,), jnp.int32)
        .at[destination]
        .set(jnp.arange(1, flat_ids.shape[0] + 1, dtype=jnp.int32))
    )
    filled = source > 0
    token_row = jnp.maximum(source - 1, 0) // TOP
    outgoing = jnp.where(filled[:, None], tokens[token_row], jnp.zeros((), jnp.bfloat16)).reshape(
        owners, CAP, tokens.shape[1]
    )
    incoming = lax.all_to_all(outgoing, "roll", split_axis=0, concat_axis=0, tiled=True).reshape(
        slot_count, tokens.shape[1]
    )
    gate_up = jnp.concatenate((dequant_gate, dequant_up), axis=0)
    projected = lax.dot_general(
        incoming, gate_up, (((1,), (1,)), ((), ())), preferred_element_type=jnp.float32
    )
    hidden = (jax.nn.silu(projected[:, :hidden_units]) * projected[:, hidden_units:]).astype(
        jnp.bfloat16
    )
    partial_value = jnp.dot(hidden, dequant_down, preferred_element_type=jnp.float32).reshape(
        owners, CAP, tokens.shape[1]
    )
    summed = lax.psum_scatter(partial_value, "train", scatter_dimension=2, tiled=True).astype(
        jnp.bfloat16
    )
    returned = lax.all_to_all(summed, "roll", split_axis=0, concat_axis=0, tiled=True)
    returned = returned.reshape(slot_count, returned.shape[2])
    picked_rows = (
        returned[destination].astype(jnp.float32).reshape(tokens.shape[0], TOP, returned.shape[1])
    )
    combined = jnp.sum(gate_weights[:, :, None] * picked_rows, axis=1).astype(jnp.bfloat16)
    return (slot_gate[None], slot_up[None], slot_down[None], combined)


def solution(mesh):
    in_specs = (
        P(None, "roll", "train"),
        P(None, "roll", "train"),
        P(None, "roll", "train"),
        P("roll", None),
        P("roll", None),
        P("roll", None),
        P(),
    )
    out_specs = (
        P("roll", None, "train", None),
        P("roll", None, "train", None),
        P("roll", None, "train", None),
        P("roll", "train"),
    )
    return jax.shard_map(
        per_device, mesh=mesh, in_specs=in_specs, out_specs=out_specs, check_vma=False
    )
```

profile of v0, /device:TPU:19, one launch (start us, length us, event | category | flops | bytes accessed | tf_op | source)
XLA Modules:
  0.0 1140.6 jit_solution(7424661183740151398)
XLA Ops:
  100.4 14.4 %broadcast_select_fusion = (bf16[8,2,128,1792]{3,2,1,0:T(8,128)(2,1)}, bf16[8,2,128,1792]{3,2,1,0:T(8,128)(2,1)}, bf16[8,2,128,1792]{3,2,1,0:T(8,128)(2,1)}) fusion(bf16[8,2,128,1792]{3,2,1,0:T(8,128)(2,1)} %gather_fusion.5, pred[8]{0:T(512)(128)(4,1)S(1)} %compare_and_fusion, bf16[8,2,128,1792]{3,2,1,0:T(8,128)(2,1)} %gather_fusion.4, ...), kind=kLoop, calls=%fused_computation.19 | loop fusion | flops 11010048 | bytes 44040200 | tf_op jit(solution)/shard_map/jit(_take)/select_n | solution.py:38
  114.9 164.3 %all_to_all.87 = bf16[8,2,128,1792]{3,2,1,0:T(8,128)(2,1)} all-to-all(bf16[8,2,128,1792]{3,2,1,0:T(8,128)(2,1)} %get-tuple-element.16), channel_id=1, replica_groups=mesh['train'=4,'roll'=8] {'roll'}, dimensions={0} | all-to-all | bytes 14680064 | tf_op jit(solution)/shard_map/all_to_all | solution.py:42
  279.2 164.9 %all_to_all.88 = bf16[8,2,128,1792]{3,2,1,0:T(8,128)(2,1)} all-to-all(bf16[8,2,128,1792]{3,2,1,0:T(8,128)(2,1)S(1)} %copy-done.2), channel_id=1, replica_groups=mesh['train'=4,'roll'=8] {'roll'}, dimensions={0} | all-to-all | bytes 14680064 | tf_op jit(solution)/shard_map/all_to_all | solution.py:41
  453.3 10.2 copy.112
  463.5 147.4 %all-to-all-done.4 = bf16[8,2,128,1792]{3,2,1,0:T(8,128)(2,1)} async-done(((bf16[8,2,128,1792]{3,2,1,0:T(8,128)(2,1)}), bf16[8,2,128,1792]{3,2,1,0:T(8,128)(2,1)}, u32[]{:S(2)}, u32[]{:S(2)}) %all-to-all-start.4) | async-done | bytes 7340064 | tf_op jit(solution)/shard_map/all_to_all | solution.py:43
  616.4 10.2 copy.106
  626.6 70.0 %all-to-all-done.3 = bf16[16,128,1792]{2,0,1:T(8,128)(2,1)} async-done(((bf16[16,128,1792]{2,0,1:T(8,128)(2,1)}), bf16[16,128,1792]{2,0,1:T(8,128)(2,1)}, u32[]{:S(2)}, u32[]{:S(2)}) %all-to-all-start.3) | async-done | bytes 7340064 | tf_op jit(solution)/shard_map/all_to_all | solution.py:54
  707.8 74.1 %all-to-all-done.1 = bf16[16,128,1792]{2,0,1:T(8,128)(2,1)} async-done(((bf16[16,128,1792]{2,0,1:T(8,128)(2,1)}), bf16[16,128,1792]{2,0,1:T(8,128)(2,1)}, u32[]{:S(2)}, u32[]{:S(2)}) %all-to-all-start.1) | async-done | bytes 7340064 | tf_op jit(solution)/shard_map/all_to_all | solution.py:51
  791.3 10.2 copy.118
  814.0 13.6 %copy.145 = f32[64,8,4,1792]{3,1,2,0:T(8,128)} copy(f32[64,8,4,1792]{3,2,1,0:T(4,128)} %bitcast.102) | data formatting | bytes 29360128
  839.9 13.5 %copy.143 = f32[64,8,4,1792]{3,1,2,0:T(8,128)} copy(f32[64,8,4,1792]{3,2,1,0:T(4,128)} %bitcast.103) | data formatting | bytes 29360128
  865.4 12.8 %fusion = bf16[512,7168]{1,0:T(8,128)(2,1)S(1)} fusion(f32[512,7168]{1,0:T(8,128)} %bitcast.96, f32[64,8,56,128]{3,2,1,0:T(8,128)} %bitcast.100), kind=kLoop, calls=%fused_computation.8 | loop fusion | flops 7340032 | bytes 36700160 | tf_op jit(solution)/shard_map/convert_element_type | solution.py:23
  884.5 10.9 fusion.1
  904.8 35.0 %all-to-all-done.5 = bf16[16,128,1792]{2,0,1:T(8,128)(2,1)} async-done(((bf16[16,128,1792]{2,0,1:T(8,128)(2,1)}), bf16[16,128,1792]{2,0,1:T(8,128)(2,1)}, u32[]{:S(2)}, u32[]{:S(2)}) %all-to-all-start.5) | async-done | bytes 7340064 | tf_op jit(solution)/shard_map/all_to_all | solution.py:57
  952.2 17.7 %reshape.283 = f32[16,32,56,128]{3,2,1,0:T(8,128)} reshape(f32[16,32,4,1792]{3,2,1,0:T(4,128)} %copy.130) | data formatting | bytes 29360128 | tf_op jit(solution)/shard_map/convert_element_type | solution.py:21
  969.9 10.0 multiply_convert_fusion
  979.9 11.7 %reshape.353 = bf16[512,7168,1]{1,0,2:T(8,128)(2,1)} reshape(bf16[16,32,56,128]{3,2,1,0:T(8,128)(2,1)} %multiply_convert_fusion) | data formatting | bytes 14680064 | tf_op jit(solution)/shard_map/convert_element_type | solution.py:23
  997.7 49.0 %reduce-scatter.2.cloned.1.call-done = f32[8,16,1792]{2,1,0:T(8,128)} async-done(((f32[8,16,7168]{2,1,0:T(8,128)}), f32[8,16,1792]{2,1,0:T(8,128)}) %reduce-scatter.2.cloned.1.call-update) | async-done | bytes 917520 | tf_op jit(solution)/shard_map/reduce_scatter | solution.py:111
  1054.2 11.8 %copy.108 = bf16[16,32,4,1792]{3,2,1,0:T(4,128)(2,1)} copy(bf16[16,32,4,1792]{3,0,1,2:T(8,128)(2,1)} %bitcast.4) | data formatting | bytes 14680064 | tf_op jit(solution)/shard_map/all_to_all | solution.py:51
  1066.0 13.5 %broadcast_in_dim.47 = bf16[1,16,32,7168]{3,2,1,0:T(8,128)(2,1)} reshape(bf16[16,32,4,1792]{3,2,1,0:T(4,128)(2,1)} %copy.108) | data formatting | bytes 14680064 | tf_op jit(solution)/shard_map/broadcast_in_dim | solution.py:120
  1079.5 11.8 %copy.114 = bf16[16,32,4,1792]{3,2,1,0:T(4,128)(2,1)} copy(bf16[16,32,4,1792]{3,0,1,2:T(8,128)(2,1)} %bitcast.9) | data formatting | bytes 14680064 | tf_op jit(solution)/shard_map/all_to_all | solution.py:54
  1091.3 13.5 %broadcast_in_dim.48 = bf16[1,16,32,7168]{3,2,1,0:T(8,128)(2,1)} reshape(bf16[16,32,4,1792]{3,2,1,0:T(4,128)(2,1)} %copy.114) | data formatting | bytes 14680064 | tf_op jit(solution)/shard_map/broadcast_in_dim | solution.py:120
  1104.9 11.8 %copy.120 = bf16[16,32,4,1792]{3,2,1,0:T(4,128)(2,1)} copy(bf16[16,32,4,1792]{3,0,1,2:T(8,128)(2,1)} %bitcast.14) | data formatting | bytes 14680064 | tf_op jit(solution)/shard_map/all_to_all | solution.py:57
  1116.6 13.3 %broadcast_in_dim.49 = bf16[1,16,32,7168]{3,2,1,0:T(8,128)(2,1)} reshape(bf16[16,32,4,1792]{3,2,1,0:T(4,128)(2,1)} %copy.120) | data formatting | bytes 14680064 | tf_op jit(solution)/shard_map/broadcast_in_dim | solution.py:120
  (116 shorter events, 210.1 us)
Async XLA Ops:
  7.2 697.5 %copy-start = (bf16[64,7168]{1,0:T(8,128)(2,1)S(1)}, bf16[64,7168]{1,0:T(8,128)(2,1)}, u32[]{:S(2)}) copy-start(bf16[64,7168]{1,0:T(8,128)(2,1)} %param.12) | copy-start | bytes 2752516
  58.0 38.0 %all-to-all-start.7 = ((bf16[8,2,14,3]{2,1,3,0:T(2,128)(2,1)}), bf16[8,2,14,3]{2,1,3,0:T(2,128)(2,1)S(1)}, u32[]{:S(2)}, u32[]{:S(2)}) async-start(bf16[8,2,14,3]{2,1,3,0:T(2,128)(2,1)} %broadcast_select_fusion.4), calls=%async_computation.7 | async-start | bytes 24576 | tf_op jit(solution)/shard_map/all_to_all | solution.py:44
  63.9 11.4 slice-start.4
  69.6 5.7 slice-start.5
  96.7 18.1 %all-to-all-start.8 = ((bf16[4,2,336]{2,1,0:T(2,128)(2,1)}), bf16[4,2,336]{2,1,0:T(2,128)(2,1)S(1)}, u32[]{:S(2)}, u32[]{:S(2)}) async-start(bf16[4,2,336]{2,1,0:T(2,128)(2,1)} %reshape.360), calls=%async_computation.8 | async-start | bytes 12288 | tf_op jit(solution)/shard_map/all_to_all | solution.py:60
  114.8 164.3 %copy-start.2 = (bf16[8,2,128,1792]{3,2,1,0:T(8,128)(2,1)S(1)}, bf16[8,2,128,1792]{3,2,1,0:T(8,128)(2,1)}, u32[]{:S(2)}) copy-start(bf16[8,2,128,1792]{3,2,1,0:T(8,128)(2,1)} %get-tuple-element.17) | copy-start | bytes 22020100
  444.1 166.9 %all-to-all-start.4 = ((bf16[8,2,128,1792]{3,2,1,0:T(8,128)(2,1)}), bf16[8,2,128,1792]{3,2,1,0:T(8,128)(2,1)}, u32[]{:S(2)}, u32[]{:S(2)}) async-start(bf16[8,2,128,1792]{3,2,1,0:T(8,128)(2,1)} %get-tuple-element.15), calls=%async_computation.4 | async-start | bytes 14680064 | tf_op jit(solution)/shard_map/all_to_all | solution.py:43
  610.9 85.7 %all-to-all-start.3 = ((bf16[16,128,1792]{2,0,1:T(8,128)(2,1)}), bf16[16,128,1792]{2,0,1:T(8,128)(2,1)}, u32[]{:S(2)}, u32[]{:S(2)}) async-start(bf16[16,128,1792]{2,0,1:T(8,128)(2,1)} %copy.112), calls=%async_computation.3 | async-start | bytes 14680064 | tf_op jit(solution)/shard_map/all_to_all | solution.py:54
  626.6 75.9 %copy-start.3 = (s32[64,2]{0,1:T(2,128)S(1)}, s32[64,2]{0,1:T(2,128)}, u32[]{:S(2)}) copy-start(s32[64,2]{0,1:T(2,128)} %param.13) | copy-start | bytes 1540
  626.6 76.4 %copy-start.5 = (s32[8]{0:T(128)S(1)}, s32[8]{0:T(128)}, u32[]{:S(2)}) copy-start(s32[8]{0:T(128)} %param.15) | copy-start | bytes 100
  696.6 85.3 %all-to-all-start.1 = ((bf16[16,128,1792]{2,0,1:T(8,128)(2,1)}), bf16[16,128,1792]{2,0,1:T(8,128)(2,1)}, u32[]{:S(2)}, u32[]{:S(2)}) async-start(bf16[16,128,1792]{2,0,1:T(8,128)(2,1)} %copy.106), calls=%async_computation.1 | async-start | bytes 14680064 | tf_op jit(solution)/shard_map/all_to_all | solution.py:51
  781.9 71.5 %all-to-all-start.6 = ((bf16[8,16,7168]{2,1,0:T(8,128)(2,1)}), bf16[8,16,7168]{2,1,0:T(8,128)(2,1)S(1)}, u32[]{:S(2)}, u32[]{:S(2)}) async-start(bf16[8,16,7168]{2,1,0:T(8,128)(2,1)} %broadcast_select_fusion.3), calls=%async_computation.6 | async-start | bytes 3670016 | tf_op jit(solution)/shard_map/all_to_all | solution.py:98
  853.5 86.3 %all-to-all-start.5 = ((bf16[16,128,1792]{2,0,1:T(8,128)(2,1)}), bf16[16,128,1792]{2,0,1:T(8,128)(2,1)}, u32[]{:S(2)}, u32[]{:S(2)}) async-start(bf16[16,128,1792]{2,0,1:T(8,128)(2,1)} %copy.118), calls=%async_computation.5 | async-start | bytes 14680064 | tf_op jit(solution)/shard_map/all_to_all | solution.py:57
  859.2 187.5 %reduce-scatter.2.cloned.1.call-start = ((), (), s32[]{:S(2)}) async-start(), calls=%async_computation.11 | async-start | bytes 4587520 | tf_op jit(solution)/shard_map/reduce_scatter | solution.py:111
  865.4 19.1 %slice-start = ((s8[14680064]{0:T(1024)(128)(4,1)}), s8[4194304]{0:T(1024)(128)(4,1)S(1)}, s32[]{:S(2)}) async-start(s8[14680064]{0:T(1024)(128)(4,1)} %bitcast.97), calls=%async_computation.12 | async-start | bytes 8388608
  865.4 19.1 %slice-start.1 = ((s8[14680064]{0:T(1024)(128)(4,1)}), s8[4194304]{0:T(1024)(128)(4,1)S(1)}, s32[]{:S(2)}) async-start(s8[14680064]{0:T(1024)(128)(4,1)} %bitcast.97), calls=%async_computation.13 | async-start | bytes 8388608
  865.4 19.1 %slice-start.2 = ((s8[14680064]{0:T(1024)(128)(4,1)}), s8[4194304]{0:T(1024)(128)(4,1)S(1)}, s32[]{:S(2)}) async-start(s8[14680064]{0:T(1024)(128)(4,1)} %bitcast.97), calls=%async_computation.14 | async-start | bytes 8388608
  878.2 6.2 slice-start.3
  991.6 62.5 %copy-start.4 = (f32[64,2]{0,1:T(2,128)S(1)}, f32[64,2]{0,1:T(2,128)}, u32[]{:S(2)}) copy-start(f32[64,2]{0,1:T(2,128)} %param.14) | copy-start | bytes 1540
  1048.7 81.3 %all-to-all-start.9 = ((bf16[8,16,1792]{2,1,0:T(8,128)(2,1)}), bf16[8,16,1792]{2,1,0:T(8,128)(2,1)S(1)}, u32[]{:S(2)}, u32[]{:S(2)}) async-start(bf16[8,16,1792]{2,1,0:T(8,128)(2,1)} %convert_element_type.214), calls=%async_computation.10 | async-start | bytes 917504 | tf_op jit(solution)/shard_map/all_to_all | solution.py:114
  1104.9 28.4 %copy-start.1 = (bf16[64,7168]{1,0:T(8,128)(2,1)S(1)}, bf16[64,7168]{1,0:T(8,128)(2,1)}, u32[]{:S(2)}) copy-start(bf16[64,7168]{1,0:T(8,128)(2,1)} %param.12) | copy-start | bytes 2752516
Sparse Core Ops, SparseCore 0:
  997.9 48.7 reduce-scatter.1
where the time goes:
time: 1150 us; the launch traced here: 1140 us
  waiting for transfers between devices  376 us (33%)
  blocking collectives  329 us (29%)
  local copies, waits for them, and re-layouts  259 us (23%)
  other arithmetic  96.2 us (8%)
  starting transfers between devices  50 us (4%)
  matrix products  15.4 us (1%)
  between operations  14.8 us (1%)
    all_to_all x1, blocking collectives, per_device(): lax.all_to_all(picked_gate, 'roll', split_axis=0, concat_axis=0, tiled=True)  165 us
    all_to_all x1, blocking collectives, per_device(): lax.all_to_all(picked_up, 'roll', split_axis=0, concat_axis=0, tiled=True)  164 us
    all_to_all x1, waiting for transfers between devices, per_device(): lax.all_to_all(picked_down, 'roll', split_axis=0, concat_axis=0, tiled=True)  147 us
    all_to_all x1, waiting for transfers between devices, per_device(): lax.all_to_all(got_gate.reshape(flat_shape), 'train', split_axis=1, conca...  74.1 us
    all_to_all x1, waiting for transfers between devices, per_device(): lax.all_to_all(got_up.reshape(flat_shape), 'train', split_axis=1, concat_...  70 us
    reduce_scatter x1, waiting for transfers between devices, per_device(): lax.psum_scatter(partial_value, 'train', scatter_dimension=2, tiled=True)  49 us
    broadcast_in_dim x3, local copies, waits for them, and re-layouts, per_device(): return (slot_gate[None], slot_up[None], slot_down[None], combined)  40.3 us
    convert_element_type x4, local copies, waits for them, and re-layouts, dequantize_slot(): quantized.astype(jnp.float32)  38.7 us
  transfers between devices with their start and end apart: 9, of which 5 were waited for; matrix products, arithmetic and copies ran while one was open for 22% of the time, Pallas kernels for 0%

commit v1 on v0

v1 whole, which is shorter than its diff:
```python
import functools

import jax
import jax.numpy as jnp
from jax import lax
from jax.experimental import pallas as pl
from jax.experimental.pallas import tpu as pltpu
from jax.sharding import PartitionSpec as P

BLOCK = 128
CORES = 2
VMEM_BYTES = 48 * 1024 * 1024


def any_spec():
    return pl.BlockSpec(memory_space=pl.ANY)


def smem_spec():
    return pl.BlockSpec(memory_space=pltpu.SMEM)


def quantize_kernel(trains, x_ref, q_ref, d_ref):
    rows = BLOCK // trains
    features = x_ref.shape[-1]
    for col in range(features // BLOCK):
        cols = slice(col * BLOCK, (col + 1) * BLOCK)
        block = x_ref[0, :, cols]
        peak = jnp.max(jnp.max(jnp.abs(block), axis=0, keepdims=True), axis=1, keepdims=True)
        scale = peak.astype(jnp.bfloat16).astype(jnp.float32)
        quant = (block * (1.0 / scale)).astype(jnp.bfloat16)
        q_ref[:, 0, 0, :, cols] = quant.reshape(trains, rows, BLOCK)
        d_ref[0, 0, :, cols] = (quant.astype(jnp.float32) * scale).astype(jnp.bfloat16)


def quantize(master, first, count, trains):
    experts, _, features = master.shape
    rows = BLOCK // trains
    return pl.pallas_call(
        functools.partial(quantize_kernel, trains),
        grid=(experts, count),
        in_specs=[pl.BlockSpec((1, BLOCK, features), lambda e, b: (e, first + b, 0))],
        out_specs=[
            pl.BlockSpec((trains, 1, 1, rows, features), lambda e, b: (0, e, b, 0, 0)),
            pl.BlockSpec((1, 1, BLOCK, features), lambda e, b: (e, b, 0, 0)),
        ],
        out_shape=[
            jax.ShapeDtypeStruct((trains, experts, count, rows, features), jnp.bfloat16),
            jax.ShapeDtypeStruct((experts, count, BLOCK, features), jnp.bfloat16),
        ],
        compiler_params=pltpu.CompilerParams(vmem_limit_bytes=VMEM_BYTES),
        cost_estimate=pl.CostEstimate(
            flops=8 * experts * count * BLOCK * features,
            bytes_accessed=8 * experts * count * BLOCK * features,
            transcendentals=0,
        ),
        name="quantize",
    )(master)


def gather_kernel(picks, plan_ref, x_ref, *refs):
    outs, sem = refs[:-1], refs[-1]
    copies = []
    for out, places in zip(outs, picks):
        for slot, place in enumerate(places):
            copies.append(
                pltpu.make_async_copy(
                    x_ref.at[:, plan_ref[place]], out.at[slot], sem.at[len(copies)]
                )
            )
    for copy in copies:
        copy.start()
    for copy in copies:
        copy.wait()


def gather_pieces(plan, x, picks):
    trains, _, count, rows, features = x.shape
    total = sum(len(places) for places in picks)
    piece = trains * count * rows * features
    return pl.pallas_call(
        functools.partial(gather_kernel, picks),
        in_specs=[smem_spec(), any_spec()],
        out_specs=[any_spec()] * len(picks),
        out_shape=[
            jax.ShapeDtypeStruct((len(places), trains, count, rows, features), x.dtype)
            for places in picks
        ],
        scratch_shapes=[pltpu.SemaphoreType.DMA((total,))],
        cost_estimate=pl.CostEstimate(
            flops=0, bytes_accessed=4 * total * piece, transcendentals=0
        ),
        name="gather_pieces",
    )(plan, x)


def pick_kernel(choices, plan_ref, *refs):
    cands, out, sem = refs[:-2], refs[-2], refs[-1]
    for cand, slot, side, place, wanted in choices:
        hit = (plan_ref[side[0]] == side[1]) & (plan_ref[place] == wanted)

        @pl.when(hit)
        def _():
            pltpu.make_async_copy(cands[cand].at[slot], out, sem).start()

    pltpu.make_async_copy(cands[0].at[0], out, sem).wait()


def pick_piece(plan, cands, choices):
    shape = cands[0].shape[1:]
    size = 1
    for dim in shape:
        size *= dim
    return pl.pallas_call(
        functools.partial(pick_kernel, choices),
        in_specs=[smem_spec()] + [any_spec()] * len(cands),
        out_specs=any_spec(),
        out_shape=jax.ShapeDtypeStruct(shape, cands[0].dtype),
        scratch_shapes=[pltpu.SemaphoreType.DMA],
        cost_estimate=pl.CostEstimate(flops=0, bytes_accessed=4 * size, transcendentals=0),
        name="pick_piece",
    )(plan, *cands)


def place_kernel(layout, plan_ref, *refs):
    own, other, sources, first, count, blocks, n_in, aliased = layout
    cands = refs[: n_in]
    out, sem = refs[n_in + aliased], refs[n_in + aliased + 1]
    trains, _, _, features = cands[own[0][0][0]].shape[-4:]

    def target(source, part):
        start = source * blocks + first
        return out.at[pl.ds(start, count), :, pl.ds(part * features, features)]

    waits = []
    for offset, choices in enumerate(own):
        source = plan_ref[sources[offset][0]]
        for cand, slot, tests in choices:
            hit = None
            for place, wanted in tests:
                test = plan_ref[place] == wanted
                hit = test if hit is None else hit & test
            piece = cands[cand]

            def go(piece=piece, slot=slot, source=source, offset=offset):
                for part in range(trains):
                    if isinstance(slot, str):
                        expert = plan_ref[int(slot)]
                        view = piece.at[part, expert]
                    else:
                        view = piece.at[slot, part]
                    pltpu.make_async_copy(
                        view, target(source, part), sem.at[2 * offset, part]
                    ).start()

            if hit is None:
                go()
            else:
                pl.when(hit)(go)
        source_other = plan_ref[sources[offset][1]]
        for part in range(trains):
            pltpu.make_async_copy(
                cands[other[offset]].at[part], target(source_other, part), sem.at[2 * offset + 1, part]
            ).start()
        waits.append(offset)
    for offset in waits:
        for part in range(trains):
            piece = cands[other[offset]].at[part]
            for side in range(2):
                pltpu.make_async_copy(
                    piece, target(0, part), sem.at[2 * offset + side, part]
                ).wait()


def place_chunk(plan, cands, own, other, sources, first, blocks, out):
    trains, count, rows, features = cands[other[0]].shape
    offsets = len(own)
    aliased = out is not None
    layout = (own, other, sources, first, count, blocks, len(cands), int(aliased))
    shape = (2 * offsets * blocks, rows, trains * features)
    operands = list(cands) + ([out] if aliased else [])
    return pl.pallas_call(
        functools.partial(place_kernel, layout),
        in_specs=[smem_spec()] + [any_spec()] * len(operands),
        out_specs=any_spec(),
        out_shape=jax.ShapeDtypeStruct(shape, jnp.bfloat16),
        scratch_shapes=[pltpu.SemaphoreType.DMA((2 * offsets, trains))],
        input_output_aliases={len(operands): 0} if aliased else {},
        cost_estimate=pl.CostEstimate(
            flops=0,
            bytes_accessed=8 * offsets * trains * count * rows * features,
            transcendentals=0,
        ),
        name="place_chunk",
    )(plan, *operands)


def make_plan(placement, experts, owners):
    chips = owners // CORES
    me = lax.axis_index("roll")
    chip, core = me // CORES, me % CORES
    expert_range = jnp.arange(experts, dtype=jnp.int32)
    owner_chip = jnp.arange(owners, dtype=jnp.int32) // CORES
    held = placement[None, :] == expert_range[:, None]
    last = jnp.max(jnp.where(held, owner_chip[None, :], -1), axis=1)
    first = jnp.min(jnp.where(held, owner_chip[None, :], chips), axis=1)

    def ranks(key):
        ahead = (key[None, :] > key[:, None]) | (
            (key[None, :] == key[:, None]) & (expert_range[None, :] < expert_range[:, None])
        )
        return jnp.sum(ahead.astype(jnp.int32), axis=1)

    rank_up, rank_down = ranks(last), ranks(-first)
    order_up = jnp.sum(
        jnp.where(rank_up[:, None] == expert_range[None, :], expert_range[:, None], 0), axis=0
    )
    order_down = jnp.sum(
        jnp.where(rank_down[:, None] == expert_range[None, :], expert_range[:, None], 0), axis=0
    )
    own = jnp.sum(jnp.where(jnp.arange(owners) == me, placement, 0))
    mate = jnp.sum(jnp.where(jnp.arange(owners) == chip * CORES + 1 - core, placement, 0))

    def at(table, expert):
        return jnp.sum(jnp.where(expert_range == expert, table, 0))

    scalars = [own, mate, at(rank_up, own), at(rank_up, mate), at(rank_down, own), at(rank_down, mate)]
    names = ["own", "mate", "up_own", "up_mate", "down_own", "down_mate"]
    for offset in range(chips):
        source = (chip + chips - offset) % chips
        scalars += [
            (chip >= offset).astype(jnp.int32),
            source * CORES + core,
            source * CORES + 1 - core,
        ]
        names += [f"side{offset}", f"from{offset}", f"mate_from{offset}"]
    places = {name: 2 * experts + i for i, name in enumerate(names)}
    plan = jnp.concatenate(
        (order_up, order_down, jnp.stack([s.astype(jnp.int32) for s in scalars]))
    ).astype(jnp.int32)
    return plan, places


def slot_links(experts, chips, tight):
    caps = [min(experts, CORES * (chips - 1 - link)) for link in range(chips - 1)]
    if tight:
        middle = chips // 2 - 1
        caps = [min(cap, experts - 1) if link >= middle else cap for link, cap in enumerate(caps)]
    return [sum(1 for cap in caps if slot < cap) for slot in range(experts)]


def slot_groups(experts, chips, tight):
    links = slot_links(experts, chips, tight)
    groups = []
    for slot in range(experts):
        if groups and links[groups[-1][0]] == links[slot]:
            groups[-1].append(slot)
        else:
            groups.append([slot])
    return [(slots, links[slots[0]]) for slots in groups]


def hop(piece, links, step, chips, up):
    pairs = []
    for link in range(step - 1, links):
        for core in range(CORES):
            if up:
                pairs.append((link * CORES + core, (link + 1) * CORES + core))
            else:
                pairs.append(
                    ((chips - 1 - link) * CORES + core, (chips - 2 - link) * CORES + core)
                )
    return lax.ppermute(piece, "roll", pairs)


def swap_cores(piece, chips):
    pairs = []
    for chip in range(chips):
        for core in range(CORES):
            pairs.append((chip * CORES + core, chip * CORES + 1 - core))
    return lax.ppermute(piece, "roll", pairs)


def hand_off(plan, places, x, chips, tight):
    experts = x.shape[1]
    groups = slot_groups(experts, chips, tight)
    picks = [[slot for slot in slots] for slots, _ in groups]
    picks += [[experts + slot for slot in slots] for slots, _ in groups]
    picks += [[places["mate"]]]
    gathered = gather_pieces(plan, x, tuple(tuple(p) for p in picks))
    n = len(groups)
    mate_piece = gathered[2 * n][0]
    moved = {}
    now = {True: list(gathered[:n]), False: list(gathered[n : 2 * n])}
    for step in range(1, chips):
        for up in (True, False):
            for g, (slots, links) in enumerate(groups):
                if links >= step:
                    now[up][g] = hop(now[up][g], links, step, chips, up)
                    moved[up, step, g] = now[up][g]
    cands = [x]
    own = [[(0, str(places["own"]), ())]]
    other = [swap_cores(mate_piece, chips)]
    for offset in range(1, chips):
        here, choices_mate, choices_own = [], [], []
        for up, step in ((True, offset), (False, chips - offset)):
            for g, (slots, links) in enumerate(groups):
                if links < step:
                    continue
                here.append(moved[up, step, g])
                for i, slot in enumerate(slots):
                    side = (places[f"side{offset}"], int(up))
                    kind = "up" if up else "down"
                    choices_mate.append((len(here) - 1, i, side, places[f"{kind}_mate"], slot))
                    choices_own.append(
                        (len(cands) + len(here) - 1, i, (side, (places[f"{kind}_own"], slot)))
                    )
        other.append(swap_cores(pick_piece(plan, here, choices_mate), chips))
        cands += here
        own.append(choices_own)
    base = len(cands)
    cands += other
    sources = [(places[f"from{o}"], places[f"mate_from{o}"]) for o in range(chips)]
    return cands, own, [base + o for o in range(chips)], sources


def select_experts(pre, onehot):
    tokens, top, experts = onehot.shape
    pre = pre.reshape(tokens, experts, -1)
    total = jnp.zeros((tokens, top, pre.shape[2]), jnp.float32)
    for expert in range(experts):
        total = total + jnp.where(onehot[:, :, expert, None], pre[:, None, expert], 0.0)
    return total


def per_device(master_gate, master_up, master_down, tokens, expert_ids, gate_weights, placement):
    trains = lax.axis_size("train")
    owners = lax.axis_size("roll")
    chips = owners // CORES
    experts, hidden_rows, features = master_gate.shape
    blocks = hidden_rows // BLOCK
    chunks = []
    for m in range(3):
        for b in range(blocks):
            chunks.append((m, b, 1))
    plan, places = make_plan(placement, experts, owners)

    masters = (master_gate, master_up, master_down)
    dequant = [[], [], []]
    outs = [None, None, None]
    for m, first, count in chunks:
        quant, restored = quantize(masters[m], first, count, trains)
        dequant[m].append(restored)
        x = lax.all_to_all(quant, "train", split_axis=0, concat_axis=0, tiled=True)
        cands, own, other, sources = hand_off(plan, places, x, chips, False)
        outs[m] = place_chunk(plan, cands, own, other, sources, first, blocks, outs[m])

    train_me = lax.axis_index("train")
    mine = lax.dynamic_slice_in_dim(tokens, train_me * features, features, axis=1)
    every = lax.all_gather(mine, "roll", axis=0, tiled=True)
    ids = lax.all_gather(expert_ids, "roll", axis=0, tiled=True)
    weights = lax.all_gather(gate_weights, "roll", axis=0, tiled=True)
    onehot = ids[:, :, None] == jnp.arange(experts, dtype=jnp.int32)
    parts = []
    for m in range(2):
        for restored in dequant[m]:
            flat = restored.reshape(-1, features)
            pre = lax.dot_general(
                every, flat, (((1,), (1,)), ((), ())), preferred_element_type=jnp.float32
            )
            parts.append(select_experts(pre, onehot))
    pre = jnp.concatenate(parts, axis=2)
    pre = lax.psum_scatter(pre, "train", scatter_dimension=0, tiled=True)
    hidden = (jax.nn.silu(pre[:, :, :hidden_rows]) * pre[:, :, hidden_rows:]).astype(jnp.bfloat16)
    hidden = lax.all_gather(hidden, "train", axis=0, tiled=True)
    mixed = jnp.zeros((every.shape[0], features), jnp.float32)
    down = jnp.concatenate(dequant[2], axis=1) if len(dequant[2]) > 1 else dequant[2][0]
    for expert in range(experts):
        mask = onehot[:, :, expert]
        routed = jnp.sum(jnp.where(mask[:, :, None], hidden, jnp.zeros((), hidden.dtype)), axis=1)
        weight = jnp.sum(jnp.where(mask, weights, 0.0), axis=1)
        value = jnp.dot(
            routed, down[expert].reshape(hidden_rows, features), preferred_element_type=jnp.float32
        )
        mixed = mixed + weight[:, None] * value
    mixed = lax.psum_scatter(mixed, "roll", scatter_dimension=0, tiled=True).astype(jnp.bfloat16)
    return (outs[0][None], outs[1][None], outs[2][None], mixed)


def solution(mesh):
    in_specs = (
        P(None, "roll", "train"),
        P(None, "roll", "train"),
        P(None, "roll", "train"),
        P("roll", None),
        P("roll", None),
        P("roll", None),
        P(),
    )
    out_specs = (
        P("roll", None, "train", None),
        P("roll", None, "train", None),
        P("roll", None, "train", None),
        P("roll", "train"),
    )
    return jax.shard_map(
        per_device, mesh=mesh, in_specs=in_specs, out_specs=out_specs, check_vma=False
    )
```

time: 1150 us -> 2430 us (2.11)
  Pallas kernels: 0 us -> 1750 us
  blocking collectives: 329 us -> 75.7 us
  local copies, waits for them, and re-layouts: 259 us -> 29.2 us
  starting transfers between devices: 50 us -> 187 us
  other arithmetic: 96.2 us -> 18.5 us
  waiting for transfers between devices: 376 us -> 324 us
    pallas_call x0 -> x36, Pallas kernels: none -> 1750 us  [the longest x6 762 us: gather_pieces(): pl.pallas_call(functools.partial(gather_kernel, picks), in_specs=[smem_sp...]
    all_to_all x2 -> x0, blocking collectives: 329 us -> none  [the longest x1 165 us: per_device(): lax.all_to_all(picked_gate, 'roll', split_axis=0, concat_axis=0, tiled=True)]
    all_to_all x8 -> x6, waiting for transfers between devices: 327 us -> 59.2 us  [per_device(): x = lax.all_to_all(quant, 'train', split_axis=0, concat_axis=0, tiled=True)]
    ppermute x0 -> x84, waiting for transfers between devices: none -> 265 us  [the longest x60 264 us: hop(): return lax.ppermute(piece, 'roll', pairs)]
    ppermute x0 -> x84, starting transfers between devices: none -> 157 us  [the longest x60 144 us: hop(): return lax.ppermute(piece, 'roll', pairs)]
    all_gather x0 -> x3, blocking collectives: none -> 75.7 us  [the longest x1 55.9 us: per_device(): weights = lax.all_gather(gate_weights, 'roll', axis=0, tiled=True)]
    all_to_all x9 -> x0, local copies, waits for them, and re-layouts: 51.8 us -> none  [the longest x2 17.2 us: per_device(): lax.all_to_all(got_gate.reshape(flat_shape), 'train', split_axis=1, conca...]
    convert_element_type x11 -> x1, local copies, waits for them, and re-layouts: 50.9 us -> 0.14 us  [per_device(): (jax.nn.silu(pre[:, :, :hidden_rows]) * pre[:, :, hidden_rows:]).astype(j...]
  transfers between devices with their start and end apart: 9 -> 93, of which waited for: 5 -> 23; matrix products, arithmetic and copies ran while one was open for 22% -> 2% of each run, Pallas kernels for 0% -> 72%
where the time goes in v1:
time: 2430 us; the launch traced here: 2410 us
  Pallas kernels  1750 us (72%)
  waiting for transfers between devices  324 us (13%)
  starting transfers between devices  187 us (8%)
  blocking collectives  75.7 us (3%)
  local copies, waits for them, and re-layouts  29.2 us (1%)
    pallas_call x6, Pallas kernels, gather_pieces(): pl.pallas_call(functools.partial(gather_kernel, picks), in_specs=[smem_sp...  762 us
    pallas_call x6, Pallas kernels, place_chunk(): pl.pallas_call(functools.partial(place_kernel, layout), in_specs=[smem_sp...  680 us
    pallas_call x18, Pallas kernels, pick_piece(): pl.pallas_call(functools.partial(pick_kernel, choices), in_specs=[smem_sp...  282 us
    ppermute x60, waiting for transfers between devices, hop(): return lax.ppermute(piece, 'roll', pairs)  264 us
    ppermute x60, starting transfers between devices, hop(): return lax.ppermute(piece, 'roll', pairs)  144 us
    all_to_all x6, waiting for transfers between devices, per_device(): x = lax.all_to_all(quant, 'train', split_axis=0, concat_axis=0, tiled=True)  59.2 us
    all_gather x1, blocking collectives, per_device(): weights = lax.all_gather(gate_weights, 'roll', axis=0, tiled=True)  55.9 us
  transfers between devices with their start and end apart: 93, of which 23 were waited for; matrix products, arithmetic and copies ran while one was open for 2% of the time, Pallas kernels for 72%

profile of v1, /device:TPU:19, one launch (start us, length us, event | category | flops | bytes accessed | tf_op | source)
XLA Modules:
  0.0 2407.9 jit_solution(15009729801066630197)
XLA Ops:
  22.4 16.6 all-to-all-done.5.x_ref.refs_0_
  147.1 126.9 %gather_pieces.11 = (bf16[2,4,1,32,1792]{4,3,2,1,0:T(8,128)(2,1)}, bf16[2,4,1,32,1792]{4,3,2,1,0:T(8,128)(2,1)}, bf16[2,4,1,32,1792]{4,3,2,1,0:T(8,128)(2,1)}, b...) custom-call(s32[26]{0:T(128)} %concatenate.9.plan_ref, ...), custom_call_target="tpu_custom_call" | custom-call | bytes 8257536 | tf_op jit(solution)/shard_map/gather_pieces/pallas_call | solution.py:81
  281.5 126.9 %gather_pieces.10 = (bf16[2,4,1,32,1792]{4,3,2,1,0:T(8,128)(2,1)}, bf16[2,4,1,32,1792]{4,3,2,1,0:T(8,128)(2,1)}, bf16[2,4,1,32,1792]{4,3,2,1,0:T(8,128)(2,1)}, b...) custom-call(s32[26]{0:T(128)} %concatenate.9.plan_ref, ...), custom_call_target="tpu_custom_call" | custom-call | bytes 8257536 | tf_op jit(solution)/shard_map/gather_pieces/pallas_call | solution.py:81
  408.5 126.9 %gather_pieces.9 = (bf16[2,4,1,32,1792]{4,3,2,1,0:T(8,128)(2,1)}, bf16[2,4,1,32,1792]{4,3,2,1,0:T(8,128)(2,1)}, bf16[2,4,1,32,1792]{4,3,2,1,0:T(8,128)(2,1)}, bf...) custom-call(s32[26]{0:T(128)} %concatenate.9.plan_ref, ...), custom_call_target="tpu_custom_call" | custom-call | bytes 8257536 | tf_op jit(solution)/shard_map/gather_pieces/pallas_call | solution.py:81
  535.5 126.9 %gather_pieces.8 = (bf16[2,4,1,32,1792]{4,3,2,1,0:T(8,128)(2,1)}, bf16[2,4,1,32,1792]{4,3,2,1,0:T(8,128)(2,1)}, bf16[2,4,1,32,1792]{4,3,2,1,0:T(8,128)(2,1)}, bf...) custom-call(s32[26]{0:T(128)} %concatenate.9.plan_ref, ...), custom_call_target="tpu_custom_call" | custom-call | bytes 8257536 | tf_op jit(solution)/shard_map/gather_pieces/pallas_call | solution.py:81
  662.4 126.9 %gather_pieces.7 = (bf16[2,4,1,32,1792]{4,3,2,1,0:T(8,128)(2,1)}, bf16[2,4,1,32,1792]{4,3,2,1,0:T(8,128)(2,1)}, bf16[2,4,1,32,1792]{4,3,2,1,0:T(8,128)(2,1)}, bf...) custom-call(s32[26]{0:T(128)} %concatenate.9.plan_ref, ...), custom_call_target="tpu_custom_call" | custom-call | bytes 8257536 | tf_op jit(solution)/shard_map/gather_pieces/pallas_call | solution.py:81
  874.3 55.9 %all-gather.1 = f32[8,64,2]{1,2,0:T(2,128)S(1)} all-gather(f32[1,64,2]{1,2,0:T(2,128)S(1)} %bitcast.123), channel_id=1, replica_groups=mesh['train'=4,'roll'=8] {'roll'}, dimensions={0}, use_global_device_ids=true | all-gather | bytes 4608 | tf_op jit(solution)/shard_map/all_gather | solution.py:362
  948.1 126.9 %gather_pieces.6 = (bf16[2,4,1,32,1792]{4,3,2,1,0:T(8,128)(2,1)}, bf16[2,4,1,32,1792]{4,3,2,1,0:T(8,128)(2,1)}, bf16[2,4,1,32,1792]{4,3,2,1,0:T(8,128)(2,1)}, bf...) custom-call(s32[26]{0:T(128)} %concatenate.9.plan_ref, bf16[4,4,1,32,1792]{4,3,2,1,0:T(8,128)(2,1)} %all-to-all-done.x_ref.refs_0_), custom_call_target="tpu_custom_call" | custom-call | bytes 8257536 | tf_op jit(solution)/shard_map/gather_pieces/pallas_call | solution.py:81
  1120.7 17.7 collective-permute-done.7.refs_2_.refs_10_
  1200.3 41.5 %collective-permute-done.62.refs_1_.refs_5_ = bf16[2,4,1,32,1792]{4,3,2,1,0:T(8,128)(2,1)} collective-permute-done((bf16[2,4,1,32,1792]{4,3,2,1,0:T(8,128)(2,1)}, bf16[2,4,1,32,1792]{4,3,2,1,0:T(8,128)(2,1)}, u32[]{:S(2)}, u32[]{:S(2)}) %collective-permute-start.62) | collective-permute-done | bytes 917536 | tf_op jit(solution)/shard_map/ppermute | solution.py:273
  1247.6 23.2 collective-permute-done.45.refs_2_.refs_6_
  1333.0 16.4 collective-permute-done.17.refs_2_.refs_6_
  1386.1 15.8 pick_piece.31
  1523.0 15.7 pick_piece.35
  1635.7 15.7 pick_piece.23
  1668.2 15.7 pick_piece.26
  1683.9 15.7 pick_piece.20
  1699.7 15.8 pick_piece.18
  1718.1 113.2 %place_chunk.10.refs_15_ = bf16[16,32,7168]{2,1,0:T(8,128)(2,1)} custom-call(s32[26]{0:T(128)} %concatenate.9.plan_ref, bf16[4,4,1,32,1792]{4,3,2,1,0:T(8,128)(2,1)} %all-to-all-done.5.x_ref.refs_0_, bf16[2,4,1,32,1792]{4,3,2,1,0:T(8,128)(2,1)} %collective-permute-done.70.refs_0_.refs_1_, ...), custom_call_target="tpu_custom_call" | custom-call | bytes 7340032 | tf_op jit(solution)/shard_map/place_chunk/pallas_call | solution.py:182
  1831.4 113.2 %place_chunk.8.refs_15_ = bf16[16,32,7168]{2,1,0:T(8,128)(2,1)} custom-call(s32[26]{0:T(128)} %concatenate.9.plan_ref, bf16[4,4,1,32,1792]{4,3,2,1,0:T(8,128)(2,1)} %all-to-all-done.3.x_ref.refs_0_, bf16[2,4,1,32,1792]{4,3,2,1,0:T(8,128)(2,1)} %collective-permute-done.42.refs_0_.refs_1_, ...), custom_call_target="tpu_custom_call" | custom-call | bytes 7340032 | tf_op jit(solution)/shard_map/place_chunk/pallas_call | solution.py:182
  1944.6 113.2 %place_chunk.6.refs_15_ = bf16[16,32,7168]{2,1,0:T(8,128)(2,1)} custom-call(s32[26]{0:T(128)} %concatenate.9.plan_ref, bf16[4,4,1,32,1792]{4,3,2,1,0:T(8,128)(2,1)} %all-to-all-done.1.x_ref.refs_0_, bf16[2,4,1,32,1792]{4,3,2,1,0:T(8,128)(2,1)} %collective-permute-done.14.refs_0_.refs_1_, ...), custom_call_target="tpu_custom_call" | custom-call | bytes 7340032 | tf_op jit(solution)/shard_map/place_chunk/pallas_call | solution.py:182
  2057.9 113.2 %place_chunk.11 = bf16[16,32,7168]{2,1,0:T(8,128)(2,1)} custom-call(s32[26]{0:T(128)} %concatenate.9.plan_ref, bf16[4,4,1,32,1792]{4,3,2,1,0:T(8,128)(2,1)} %all-to-all-done.4.x_ref.refs_0_, bf16[2,4,1,32,1792]{4,3,2,1,0:T(8,128)(2,1)} %collective-permute-done.56.refs_0_.refs_1_, ...), custom_call_target="tpu_custom_call", output_to_operand_aliasing={{}: (16, {})} | custom-call | bytes 7340032 | tf_op jit(solution)/shard_map/place_chunk/pallas_call | solution.py:182
  2171.1 113.2 %place_chunk.9 = bf16[16,32,7168]{2,1,0:T(8,128)(2,1)} custom-call(s32[26]{0:T(128)} %concatenate.9.plan_ref, bf16[4,4,1,32,1792]{4,3,2,1,0:T(8,128)(2,1)} %all-to-all-done.2.x_ref.refs_0_, bf16[2,4,1,32,1792]{4,3,2,1,0:T(8,128)(2,1)} %collective-permute-done.28.refs_0_.refs_1_, ...), custom_call_target="tpu_custom_call", output_to_operand_aliasing={{}: (16, {})} | custom-call | bytes 7340032 | tf_op jit(solution)/shard_map/place_chunk/pallas_call | solution.py:182
  2286.3 113.4 %place_chunk.7 = bf16[16,32,7168]{2,1,0:T(8,128)(2,1)} custom-call(s32[26]{0:T(128)} %concatenate.9.plan_ref, bf16[4,4,1,32,1792]{4,3,2,1,0:T(8,128)(2,1)} %all-to-all-done.x_ref.refs_0_, bf16[2,4,1,32,1792]{4,3,2,1,0:T(8,128)(2,1)} %collective-permute-done.refs_0_.refs_1_, bf16[2,4,1,32,1792]{4,3,2,1,0:T(8,128)(2,1)} %copy-done.28, ...), custom_call_target="tpu_custom_call", output_to_operand_aliasing={{}: (16, {})} | custom-call | bytes 7340032 | tf_op jit(solution)/shard_map/place_chunk/pallas_call | solution.py:182
  (374 shorter events, 685.0 us)
Async XLA Ops:
  69.7 719.6 %all-gather.4.cloned.1.call-start = ((), (), s32[]{:S(2)}) async-start(), calls=%async_computation.7 | async-start | bytes 2064384 | tf_op jit(solution)/shard_map/all_gather | solution.py:360
  116.1 546.3 %all-to-all-start.1 = ((bf16[4,4,1,32,1792]{4,3,2,1,0:T(8,128)(2,1)}), bf16[4,4,1,32,1792]{4,3,2,1,0:T(8,128)(2,1)}, u32[]{:S(2)}, u32[]{:S(2)}) async-start(bf16[4,4,1,32,1792]{4,3,2,1,0:T(8,128)(2,1)} %copy-done.4), calls=%async_computation.1 | async-start | bytes 3670016 | tf_op jit(solution)/shard_map/all_to_all | solution.py:354
  121.8 966.3 %all-reduce.3.cloned.1.call-start = ((), (), s32[]{:S(2)}) async-start(), calls=%async_computation.9 | async-start | bytes 4194304
  274.0 534.3 %collective-permute-start.72 = (bf16[2,4,1,32,1792]{4,3,2,1,0:T(8,128)(2,1)}, bf16[2,4,1,32,1792]{4,3,2,1,0:T(8,128)(2,1)S(1)}, u32[]{:S(2)}, u32[]{:S(2)}) collective-permute-start(bf16[2,4,1,32,1792]{4,3,2,1,0:T(8,128)(2,1)} %get-tuple-element.79), channel_id=1, source_target_pairs={{6,4},{7,5},{4,2},{5,3},{2,0},{3,1},{14,12},{15,13},{12,10},{13,11... | collective-permute-start | bytes 2752520 | tf_op jit(solution)/shard_map/ppermute | solution.py:273
  276.1 536.5 %collective-permute-start.70 = (bf16[2,4,1,32,1792]{4,3,2,1,0:T(8,128)(2,1)}, bf16[2,4,1,32,1792]{4,3,2,1,0:T(8,128)(2,1)}, u32[]{:S(2)}, u32[]{:S(2)}) collective-permute-start(bf16[2,4,1,32,1792]{4,3,2,1,0:T(8,128)(2,1)} %get-tuple-element.77), channel_id=1, source_target_pairs={{0,2},{1,3},{2,4},{3,5},{4,6},{5,7},{8,10},{9,11},{10,12},{11,13},... | collective-permute-start | bytes 2752520 | tf_op jit(solution)/shard_map/ppermute | solution.py:273
  279.4 534.5 %collective-permute-start.71 = (bf16[2,4,1,32,1792]{4,3,2,1,0:T(8,128)(2,1)}, bf16[2,4,1,32,1792]{4,3,2,1,0:T(8,128)(2,1)}, u32[]{:S(2)}, u32[]{:S(2)}) collective-permute-start(bf16[2,4,1,32,1792]{4,3,2,1,0:T(8,128)(2,1)} %get-tuple-element.78), channel_id=1, source_target_pairs={{0,2},{1,3},{2,4},{3,5},{8,10},{9,11},{10,12},{11,13},{16,18},{17,... | collective-permute-start | bytes 2752520 | tf_op jit(solution)/shard_map/ppermute | solution.py:273
  280.7 514.9 %collective-permute-start.80 = (bf16[4,1,32,1792]{3,2,1,0:T(8,128)(2,1)}, bf16[4,1,32,1792]{3,2,1,0:T(8,128)(2,1)}, u32[]{:S(2)}, u32[]{:S(2)}) collective-permute-start(bf16[4,1,32,1792]{3,2,1,0:T(8,128)(2,1)} %bitcast.128), channel_id=1, source_target_pairs={{0,1},{1,0},{2,3},{3,2},{4,5},{5,4},{6,7},{7,6},{8,9},{9,8},{10,11... | collective-permute-start | bytes 1376264 | tf_op jit(solution)/shard_map/ppermute | solution.py:281
  408.4 391.7 %collective-permute-start.66 = (bf16[4,1,32,1792]{3,2,1,0:T(8,128)(2,1)}, bf16[4,1,32,1792]{3,2,1,0:T(8,128)(2,1)S(1)}, u32[]{:S(2)}, u32[]{:S(2)}) collective-permute-start(bf16[4,1,32,1792]{3,2,1,0:T(8,128)(2,1)} %bitcast.126), channel_id=1, source_target_pairs={{0,1},{1,0},{2,3},{3,2},{4,5},{5,4},{6,7},{7,6},{8,9},{9,8},{10,11... | collective-permute-start | bytes 1376264 | tf_op jit(solution)/shard_map/ppermute | solution.py:281
  826.4 106.8 %collective-permute-start.44 = (bf16[2,4,1,32,1792]{4,3,2,1,0:T(8,128)(2,1)}, bf16[2,4,1,32,1792]{4,3,2,1,0:T(8,128)(2,1)}, u32[]{:S(2)}, u32[]{:S(2)}) collective-permute-start(bf16[2,4,1,32,1792]{4,3,2,1,0:T(8,128)(2,1)} %get-tuple-element.67), channel_id=1, source_target_pairs={{6,4},{7,5},{4,2},{5,3},{2,0},{3,1},{14,12},{15,13},{12,10},{13,11... | collective-permute-start | bytes 2752520 | tf_op jit(solution)/shard_map/ppermute | solution.py:273
  874.2 1525.5 %reduce-scatter.2.cloned.1.call-start = ((), (), s32[]{:S(2)}) async-start(), calls=%async_computation.8 | async-start | bytes 4128768 | tf_op jit(solution)/shard_map/reduce_scatter | solution.py:386
  933.2 141.9 %collective-permute-start.28 = (bf16[2,4,1,32,1792]{4,3,2,1,0:T(8,128)(2,1)}, bf16[2,4,1,32,1792]{4,3,2,1,0:T(8,128)(2,1)}, u32[]{:S(2)}, u32[]{:S(2)}) collective-permute-start(bf16[2,4,1,32,1792]{4,3,2,1,0:T(8,128)(2,1)} %get-tuple-element.59), channel_id=1, source_target_pairs={{0,2},{1,3},{2,4},{3,5},{4,6},{5,7},{8,10},{9,11},{10,12},{11,13},... | collective-permute-start | bytes 2752520 | tf_op jit(solution)/shard_map/ppermute | solution.py:273
  935.1 141.3 %collective-permute-start.29 = (bf16[2,4,1,32,1792]{4,3,2,1,0:T(8,128)(2,1)}, bf16[2,4,1,32,1792]{4,3,2,1,0:T(8,128)(2,1)}, u32[]{:S(2)}, u32[]{:S(2)}) collective-permute-start(bf16[2,4,1,32,1792]{4,3,2,1,0:T(8,128)(2,1)} %get-tuple-element.60), channel_id=1, source_target_pairs={{0,2},{1,3},{2,4},{3,5},{8,10},{9,11},{10,12},{11,13},{16,18},{17,... | collective-permute-start | bytes 2752520 | tf_op jit(solution)/shard_map/ppermute | solution.py:273
  936.4 144.0 %collective-permute-start.35 = (bf16[2,4,1,32,1792]{4,3,2,1,0:T(8,128)(2,1)}, bf16[2,4,1,32,1792]{4,3,2,1,0:T(8,128)(2,1)}, u32[]{:S(2)}, u32[]{:S(2)}) collective-permute-start(bf16[2,4,1,32,1792]{4,3,2,1,0:T(8,128)(2,1)} %get-tuple-element.62), channel_id=1, source_target_pairs={{6,4},{7,5},{4,2},{5,3},{14,12},{15,13},{12,10},{13,11},{22,20},{2... | collective-permute-start | bytes 2752520 | tf_op jit(solution)/shard_map/ppermute | solution.py:273
  940.4 142.2 %collective-permute-start.16 = (bf16[2,4,1,32,1792]{4,3,2,1,0:T(8,128)(2,1)}, bf16[2,4,1,32,1792]{4,3,2,1,0:T(8,128)(2,1)}, u32[]{:S(2)}, u32[]{:S(2)}) collective-permute-start(bf16[2,4,1,32,1792]{4,3,2,1,0:T(8,128)(2,1)} %get-tuple-element.55), channel_id=1, source_target_pairs={{6,4},{7,5},{4,2},{5,3},{2,0},{3,1},{14,12},{15,13},{12,10},{13,11... | collective-permute-start | bytes 2752520 | tf_op jit(solution)/shard_map/ppermute | solution.py:273
  942.4 143.3 %collective-permute-start.14 = (bf16[2,4,1,32,1792]{4,3,2,1,0:T(8,128)(2,1)}, bf16[2,4,1,32,1792]{4,3,2,1,0:T(8,128)(2,1)}, u32[]{:S(2)}, u32[]{:S(2)}) collective-permute-start(bf16[2,4,1,32,1792]{4,3,2,1,0:T(8,128)(2,1)} %get-tuple-element.53), channel_id=1, source_target_pairs={{0,2},{1,3},{2,4},{3,5},{4,6},{5,7},{8,10},{9,11},{10,12},{11,13},... | collective-permute-start | bytes 2752520 | tf_op jit(solution)/shard_map/ppermute | solution.py:273
  1178.7 92.1 %collective-permute-start.45 = (bf16[2,4,1,32,1792]{4,3,2,1,0:T(8,128)(2,1)}, bf16[2,4,1,32,1792]{4,3,2,1,0:T(8,128)(2,1)}, u32[]{:S(2)}, u32[]{:S(2)}) collective-permute-start(bf16[2,4,1,32,1792]{4,3,2,1,0:T(8,128)(2,1)} %collective-permute-done.44.refs_1_.refs_9_), channel_id=1, source_target_pairs={{4,2},{5,3},{2,0},{3,1},{12,10},{13,11},{10,8},{11,9},{20,18},{21,... | collective-permute-start | bytes 2752520 | tf_op jit(solution)/shard_map/ppermute | solution.py:273
  1464.8 105.3 %collective-permute-start.37 = (bf16[2,4,1,32,1792]{4,3,2,1,0:T(8,128)(2,1)}, bf16[2,4,1,32,1792]{4,3,2,1,0:T(8,128)(2,1)S(1)}, u32[]{:S(2)}, u32[]{:S(2)}) collective-permute-start(bf16[2,4,1,32,1792]{4,3,2,1,0:T(8,128)(2,1)} %collective-permute-done.33.refs_0_.refs_4_), channel_id=1, source_target_pairs={{4,6},{5,7},{12,14},{13,15},{20,22},{21,23},{28,30},{29,31}} | collective-permute-start | bytes 2752520 | tf_op jit(solution)/shard_map/ppermute | solution.py:273
  1506.4 113.2 %collective-permute-start.4 = (bf16[2,4,1,32,1792]{4,3,2,1,0:T(8,128)(2,1)}, bf16[2,4,1,32,1792]{4,3,2,1,0:T(8,128)(2,1)S(1)}, u32[]{:S(2)}, u32[]{:S(2)}) collective-permute-start(bf16[2,4,1,32,1792]{4,3,2,1,0:T(8,128)(2,1)} %collective-permute-done.3.refs_2_.refs_6_), channel_id=1, source_target_pairs={{2,0},{3,1},{10,8},{11,9},{18,16},{19,17},{26,24},{27,25}} | collective-permute-start | bytes 2752520 | tf_op jit(solution)/shard_map/ppermute | solution.py:273
  1619.5 95.9 %collective-permute-start.53 = (bf16[4,1,32,1792]{3,2,1,0:T(8,128)(2,1)}, bf16[4,1,32,1792]{3,2,1,0:T(8,128)(2,1)S(1)}, u32[]{:S(2)}, u32[]{:S(2)}) collective-permute-start(bf16[4,1,32,1792]{3,2,1,0:T(8,128)(2,1)} %pick_piece.27), channel_id=1, source_target_pairs={{0,1},{1,0},{2,3},{3,2},{4,5},{5,4},{6,7},{7,6},{8,9},{9,8},{10,11... | collective-permute-start | bytes 1376264 | tf_op jit(solution)/shard_map/ppermute | solution.py:281
  1716.3 568.1 %collective-permute-start.10 = (bf16[4,1,32,1792]{3,2,1,0:T(8,128)(2,1)}, bf16[4,1,32,1792]{3,2,1,0:T(8,128)(2,1)S(1)}, u32[]{:S(2)}, u32[]{:S(2)}) collective-permute-start(bf16[4,1,32,1792]{3,2,1,0:T(8,128)(2,1)} %bitcast.18), channel_id=1, source_target_pairs={{0,1},{1,0},{2,3},{3,2},{4,5},{5,4},{6,7},{7,6},{8,9},{9,8},{10,11... | collective-permute-start | bytes 1376264 | tf_op jit(solution)/shard_map/ppermute | solution.py:281
  1716.4 454.7 %collective-permute-start.41 = (bf16[4,1,32,1792]{3,2,1,0:T(8,128)(2,1)}, bf16[4,1,32,1792]{3,2,1,0:T(8,128)(2,1)}, u32[]{:S(2)}, u32[]{:S(2)}) collective-permute-start(bf16[4,1,32,1792]{3,2,1,0:T(8,128)(2,1)} %pick_piece.26), channel_id=1, source_target_pairs={{0,1},{1,0},{2,3},{3,2},{4,5},{5,4},{6,7},{7,6},{8,9},{9,8},{10,11... | collective-permute-start | bytes 1376264 | tf_op jit(solution)/shard_map/ppermute | solution.py:281
  1717.2 567.3 %collective-permute-start.12 = (bf16[4,1,32,1792]{3,2,1,0:T(8,128)(2,1)S(1)}, bf16[4,1,32,1792]{3,2,1,0:T(8,128)(2,1)S(1)}, u32[]{:S(2)}, u32[]{:S(2)}) collective-permute-start(bf16[4,1,32,1792]{3,2,1,0:T(8,128)(2,1)S(1)} %copy-done.37), channel_id=1, source_target_pairs={{0,1},{1,0},{2,3},{3,2},{4,5},{5,4},{6,7},{7,6},{8,9},{9,8},{10,11... | collective-permute-start | bytes 1376264 | tf_op jit(solution)/shard_map/ppermute | solution.py:281
  1717.6 566.8 %collective-permute-start.13 = (bf16[4,1,32,1792]{3,2,1,0:T(8,128)(2,1)S(1)}, bf16[4,1,32,1792]{3,2,1,0:T(8,128)(2,1)S(1)}, u32[]{:S(2)}, u32[]{:S(2)}) collective-permute-start(bf16[4,1,32,1792]{3,2,1,0:T(8,128)(2,1)S(1)} %copy-done.48), channel_id=1, source_target_pairs={{0,1},{1,0},{2,3},{3,2},{4,5},{5,4},{6,7},{7,6},{8,9},{9,8},{10,11... | collective-permute-start | bytes 1376264 | tf_op jit(solution)/shard_map/ppermute | solution.py:281
  1717.7 566.7 %collective-permute-start.11 = (bf16[4,1,32,1792]{3,2,1,0:T(8,128)(2,1)}, bf16[4,1,32,1792]{3,2,1,0:T(8,128)(2,1)S(1)}, u32[]{:S(2)}, u32[]{:S(2)}) collective-permute-start(bf16[4,1,32,1792]{3,2,1,0:T(8,128)(2,1)} %pick_piece.18), channel_id=1, source_target_pairs={{0,1},{1,0},{2,3},{3,2},{4,5},{5,4},{6,7},{7,6},{8,9},{9,8},{10,11... | collective-permute-start | bytes 1376264 | tf_op jit(solution)/shard_map/ppermute | solution.py:281
  (132 other events, 5170.8 us)
Sparse Core Ops, SparseCore 0:
  72.8 28.9 all-gather.3
  822.8 85.1 all-reduce.2
  1185.1 75.4 reduce-scatter.1

commit v2 on v1

--- a/solution.py
+++ b/solution.py
@@ -59,19 +59,22 @@
 
 
 def gather_kernel(picks, plan_ref, x_ref, *refs):
-    outs, sem = refs[:-1], refs[-1]
-    copies = []
+    outs, (held, sem_in, sem_out) = refs[:-3], refs[-3:]
+    loads, stores = [], []
     for out, places in zip(outs, picks):
         for slot, place in enumerate(places):
-            copies.append(
-                pltpu.make_async_copy(
-                    x_ref.at[:, plan_ref[place]], out.at[slot], sem.at[len(copies)]
-                )
+            n = len(loads)
+            loads.append(
+                pltpu.make_async_copy(x_ref.at[:, plan_ref[place]], held.at[n], sem_in.at[n])
             )
-    for copy in copies:
-        copy.start()
-    for copy in copies:
-        copy.wait()
+            stores.append(pltpu.make_async_copy(held.at[n], out.at[slot], sem_out.at[n]))
+    for load in loads:
+        load.start()
+    for load, store in zip(loads, stores):
+        load.wait()
+        store.start()
+    for store in stores:
+        store.wait()
 
 
 def gather_pieces(plan, x, picks):
@@ -86,7 +89,12 @@
             jax.ShapeDtypeStruct((len(places), trains, count, rows, features), x.dtype)
             for places in picks
         ],
-        scratch_shapes=[pltpu.SemaphoreType.DMA((total,))],
+        scratch_shapes=[
+            pltpu.VMEM((total, trains, count, rows, features), x.dtype),
+            pltpu.SemaphoreType.DMA((total,)),
+            pltpu.SemaphoreType.DMA((total,)),
+        ],
+        compiler_params=pltpu.CompilerParams(vmem_limit_bytes=VMEM_BYTES),
         cost_estimate=pl.CostEstimate(
             flops=0, bytes_accessed=4 * total * piece, transcendentals=0
         ),
@@ -95,15 +103,18 @@
 
 
 def pick_kernel(choices, plan_ref, *refs):
-    cands, out, sem = refs[:-2], refs[-2], refs[-1]
+    cands, (out, held, sem) = refs[:-3], refs[-3:]
     for cand, slot, side, place, wanted in choices:
         hit = (plan_ref[side[0]] == side[1]) & (plan_ref[place] == wanted)
 
         @pl.when(hit)
         def _():
-            pltpu.make_async_copy(cands[cand].at[slot], out, sem).start()
-
-    pltpu.make_async_copy(cands[0].at[0], out, sem).wait()
+            pltpu.make_async_copy(cands[cand].at[slot], held, sem.at[0]).start()
+
+    pltpu.make_async_copy(cands[0].at[0], held, sem.at[0]).wait()
+    store = pltpu.make_async_copy(held, out, sem.at[1])
+    store.start()
+    store.wait()
 
 
 def pick_piece(plan, cands, choices):
@@ -116,7 +127,11 @@
         in_specs=[smem_spec()] + [any_spec()] * len(cands),
         out_specs=any_spec(),
         out_shape=jax.ShapeDtypeStruct(shape, cands[0].dtype),
-        scratch_shapes=[pltpu.SemaphoreType.DMA],
+        scratch_shapes=[
+            pltpu.VMEM(shape, cands[0].dtype),
+            pltpu.SemaphoreType.DMA((2,)),
+        ],
+        compiler_params=pltpu.CompilerParams(vmem_limit_bytes=VMEM_BYTES),
         cost_estimate=pl.CostEstimate(flops=0, bytes_accessed=4 * size, transcendentals=0),
         name="pick_piece",
     )(plan, *cands)
@@ -124,52 +139,47 @@
 
 def place_kernel(layout, plan_ref, *refs):
     own, other, sources, first, count, blocks, n_in, aliased = layout
-    cands = refs[: n_in]
-    out, sem = refs[n_in + aliased], refs[n_in + aliased + 1]
-    trains, _, _, features = cands[own[0][0][0]].shape[-4:]
-
-    def target(source, part):
-        start = source * blocks + first
-        return out.at[pl.ds(start, count), :, pl.ds(part * features, features)]
-
-    waits = []
+    cands = refs[:n_in]
+    out, held, sem_in, sem_out = refs[n_in + aliased :]
+    trains, _, _, features = cands[other[0]].shape
+
     for offset, choices in enumerate(own):
-        source = plan_ref[sources[offset][0]]
         for cand, slot, tests in choices:
             hit = None
             for place, wanted in tests:
                 test = plan_ref[place] == wanted
                 hit = test if hit is None else hit & test
-            piece = cands[cand]
-
-            def go(piece=piece, slot=slot, source=source, offset=offset):
-                for part in range(trains):
-                    if isinstance(slot, str):
-                        expert = plan_ref[int(slot)]
-                        view = piece.at[part, expert]
-                    else:
-                        view = piece.at[slot, part]
-                    pltpu.make_async_copy(
-                        view, target(source, part), sem.at[2 * offset, part]
-                    ).start()
+            if isinstance(slot, str):
+                view = cands[cand].at[:, plan_ref[int(slot)]]
+            else:
+                view = cands[cand].at[slot]
+
+            def go(view=view, offset=offset):
+                pltpu.make_async_copy(view, held.at[2 * offset], sem_in.at[2 * offset]).start()
 
             if hit is None:
                 go()
             else:
                 pl.when(hit)(go)
-        source_other = plan_ref[sources[offset][1]]
-        for part in range(trains):
-            pltpu.make_async_copy(
-                cands[other[offset]].at[part], target(source_other, part), sem.at[2 * offset + 1, part]
-            ).start()
-        waits.append(offset)
-    for offset in waits:
-        for part in range(trains):
-            piece = cands[other[offset]].at[part]
-            for side in range(2):
-                pltpu.make_async_copy(
-                    piece, target(0, part), sem.at[2 * offset + side, part]
-                ).wait()
+        pltpu.make_async_copy(
+            cands[other[offset]], held.at[2 * offset + 1], sem_in.at[2 * offset + 1]
+        ).start()
+    stores = []
+    for offset in range(len(own)):
+        for side in range(2):
+            n = 2 * offset + side
+            pltpu.make_async_copy(cands[other[0]], held.at[n], sem_in.at[n]).wait()
+            start = plan_ref[sources[offset][side]] * blocks + first
+            for part in range(trains):
+                store = pltpu.make_async_copy(
+                    held.at[n, part],
+                    out.at[pl.ds(start, count), :, pl.ds(part * features, features)],
+                    sem_out.at[n, part],
+                )
+                store.start()
+                stores.append(store)
+    for store in stores:
+        store.wait()
 
 
 def place_chunk(plan, cands, own, other, sources, first, blocks, out):
@@ -184,8 +194,13 @@
         in_specs=[smem_spec()] + [any_spec()] * len(operands),
         out_specs=any_spec(),
         out_shape=jax.ShapeDtypeStruct(shape, jnp.bfloat16),
-        scratch_shapes=[pltpu.SemaphoreType.DMA((2 * offsets, trains))],
+        scratch_shapes=[
+            pltpu.VMEM((2 * offsets, trains, count, rows, features), jnp.bfloat16),
+            pltpu.SemaphoreType.DMA((2 * offsets,)),
+            pltpu.SemaphoreType.DMA((2 * offsets, trains)),
+        ],
         input_output_aliases={len(operands): 0} if aliased else {},
+        compiler_params=pltpu.CompilerParams(vmem_limit_bytes=VMEM_BYTES),
         cost_estimate=pl.CostEstimate(
             flops=0,
             bytes_accessed=8 * offsets * trains * count * rows * features,

time: 2430 us -> 892 us (0.37)
  Pallas kernels: 1750 us -> 99.9 us
  waiting for transfers between devices: 324 us -> 434 us
    pallas_call x6, Pallas kernels: 762 us -> 21.7 us  [gather_pieces(): pl.pallas_call(functools.partial(gather_kernel, picks), in_specs=[smem_sp...]
    pallas_call x6, Pallas kernels: 680 us -> 23.2 us  [place_chunk(): pl.pallas_call(functools.partial(place_kernel, layout), in_specs=[smem_sp...]
    pallas_call x18, Pallas kernels: 282 us -> 34.1 us  [pick_piece(): pl.pallas_call(functools.partial(pick_kernel, choices), in_specs=[smem_sp...]
    ppermute x60, waiting for transfers between devices: 264 us -> 375 us  [hop(): return lax.ppermute(piece, 'roll', pairs)]
  transfers between devices with their start and end apart: 93 -> 93, of which waited for: 23 -> 36; matrix products, arithmetic and copies ran while one was open for 2% -> 4% of each run, Pallas kernels for 72% -> 11%
where the time goes in v2:
time: 892 us; the launch traced here: 888 us
  waiting for transfers between devices  434 us (49%)
  starting transfers between devices  181 us (20%)
  Pallas kernels  99.9 us (11%)
  blocking collectives  76.2 us (9%)
  local copies, waits for them, and re-layouts  50.7 us (6%)
  other arithmetic  18.4 us (2%)
  between operations  16.3 us (2%)
  matrix products  11.3 us (1%)
    ppermute x60, waiting for transfers between devices, hop(): return lax.ppermute(piece, 'roll', pairs)  375 us
    ppermute x60, starting transfers between devices, hop(): return lax.ppermute(piece, 'roll', pairs)  136 us
    all_to_all x6, waiting for transfers between devices, per_device(): x = lax.all_to_all(quant, 'train', split_axis=0, concat_axis=0, tiled=True)  57.6 us
    all_gather x1, blocking collectives, per_device(): weights = lax.all_gather(gate_weights, 'roll', axis=0, tiled=True)  56.8 us
    unnamed x192, local copies, waits for them, and re-layouts  41.4 us
    pallas_call x18, Pallas kernels, pick_piece(): pl.pallas_call(functools.partial(pick_kernel, choices), in_specs=[smem_sp...  34.1 us
    all_to_all x6, starting transfers between devices, per_device(): x = lax.all_to_all(quant, 'train', split_axis=0, concat_axis=0, tiled=True)  28.5 us
    pallas_call x6, Pallas kernels, place_chunk(): pl.pallas_call(functools.partial(place_kernel, layout), in_specs=[smem_sp...  23.2 us
  transfers between devices with their start and end apart: 93, of which 36 were waited for; matrix products, arithmetic and copies ran while one was open for 4% of the time, Pallas kernels for 11%

profile of v2, /device:TPU:19, one launch (start us, length us, event | category | flops | bytes accessed | tf_op | source)
XLA Modules:
  0.0 887.7 jit_solution(6170570130691051581)
XLA Ops:
  22.9 15.1 %all-to-all-done.5.x_ref.refs_0_ = bf16[4,4,1,32,1792]{4,3,2,1,0:T(8,128)(2,1)S(1)} async-done(((bf16[4,4,1,32,1792]{4,3,2,1,0:T(8,128)(2,1)}), bf16[4,4,1,32,1792]{4,3,2,1,0:T(8,128)(2,1)S(1)}, u32[]{:S(2)}, u32[]{:S(2)}) %all-to-all-start.5) | async-done | bytes 1835040 | tf_op jit(solution)/shard_map/all_to_all | solution.py:369
  49.3 14.4 %all-to-all-done.4.x_ref.refs_0_ = bf16[4,4,1,32,1792]{4,3,2,1,0:T(8,128)(2,1)S(1)} async-done(((bf16[4,4,1,32,1792]{4,3,2,1,0:T(8,128)(2,1)}), bf16[4,4,1,32,1792]{4,3,2,1,0:T(8,128)(2,1)S(1)}, u32[]{:S(2)}, u32[]{:S(2)}) %all-to-all-start.4) | async-done | bytes 1835040 | tf_op jit(solution)/shard_map/all_to_all | solution.py:369
  75.9 13.7 %all-to-all-done.3.x_ref.refs_0_ = bf16[4,4,1,32,1792]{4,3,2,1,0:T(8,128)(2,1)} async-done(((bf16[4,4,1,32,1792]{4,3,2,1,0:T(8,128)(2,1)}), bf16[4,4,1,32,1792]{4,3,2,1,0:T(8,128)(2,1)}, u32[]{:S(2)}, u32[]{:S(2)}) %all-to-all-start.3) | async-done | bytes 1835040 | tf_op jit(solution)/shard_map/all_to_all | solution.py:369
  101.1 14.5 %all-to-all-done.2.x_ref.refs_0_ = bf16[4,4,1,32,1792]{4,3,2,1,0:T(8,128)(2,1)} async-done(((bf16[4,4,1,32,1792]{4,3,2,1,0:T(8,128)(2,1)}), bf16[4,4,1,32,1792]{4,3,2,1,0:T(8,128)(2,1)}, u32[]{:S(2)}, u32[]{:S(2)}) %all-to-all-start.2) | async-done | bytes 1835040 | tf_op jit(solution)/shard_map/all_to_all | solution.py:369
  216.2 15.6 %collective-permute-done.58.refs_1_.refs_9_ = bf16[2,4,1,32,1792]{4,3,2,1,0:T(8,128)(2,1)} collective-permute-done((bf16[2,4,1,32,1792]{4,3,2,1,0:T(8,128)(2,1)}, bf16[2,4,1,32,1792]{4,3,2,1,0:T(8,128)(2,1)}, u32[]{:S(2)}, u32[]{:S(2)}) %collective-permute-start.58) | collective-permute-done | bytes 917536 | tf_op jit(solution)/shard_map/ppermute | solution.py:288
  259.1 56.8 %all-gather.1 = f32[8,64,2]{1,2,0:T(2,128)S(1)} all-gather(f32[1,64,2]{1,2,0:T(2,128)S(1)} %bitcast.124), channel_id=1, replica_groups=mesh['train'=4,'roll'=8] {'roll'}, dimensions={0}, use_global_device_ids=true | all-gather | bytes 4608 | tf_op jit(solution)/shard_map/all_gather | solution.py:377
  344.3 18.4 %collective-permute-done.29.refs_1_.refs_2_ = bf16[2,4,1,32,1792]{4,3,2,1,0:T(8,128)(2,1)} collective-permute-done((bf16[2,4,1,32,1792]{4,3,2,1,0:T(8,128)(2,1)}, bf16[2,4,1,32,1792]{4,3,2,1,0:T(8,128)(2,1)}, u32[]{:S(2)}, u32[]{:S(2)}) %collective-permute-start.29) | collective-permute-done | bytes 917536 | tf_op jit(solution)/shard_map/ppermute | solution.py:288
  370.9 11.5 %collective-permute-done.14.refs_0_.refs_1_ = bf16[2,4,1,32,1792]{4,3,2,1,0:T(8,128)(2,1)} collective-permute-done((bf16[2,4,1,32,1792]{4,3,2,1,0:T(8,128)(2,1)}, bf16[2,4,1,32,1792]{4,3,2,1,0:T(8,128)(2,1)}, u32[]{:S(2)}, u32[]{:S(2)}) %collective-permute-start.14) | collective-permute-done | bytes 917536 | tf_op jit(solution)/shard_map/ppermute | solution.py:288
  407.4 14.3 %collective-permute-done.refs_0_.refs_1_ = bf16[2,4,1,32,1792]{4,3,2,1,0:T(8,128)(2,1)S(1)} collective-permute-done((bf16[2,4,1,32,1792]{4,3,2,1,0:T(8,128)(2,1)}, bf16[2,4,1,32,1792]{4,3,2,1,0:T(8,128)(2,1)S(1)}, u32[]{:S(2)}, u32[]{:S(2)}) %collective-permute-start) | collective-permute-done | bytes 917536 | tf_op jit(solution)/shard_map/ppermute | solution.py:288
  446.0 14.9 %collective-permute-done.75.refs_0_.refs_4_ = bf16[2,4,1,32,1792]{4,3,2,1,0:T(8,128)(2,1)S(1)} collective-permute-done((bf16[2,4,1,32,1792]{4,3,2,1,0:T(8,128)(2,1)}, bf16[2,4,1,32,1792]{4,3,2,1,0:T(8,128)(2,1)S(1)}, u32[]{:S(2)}, u32[]{:S(2)}) %collective-permute-start.75) | collective-permute-done | bytes 917536 | tf_op jit(solution)/shard_map/ppermute | solution.py:288
  463.1 17.4 %collective-permute-done.76.refs_1_.refs_5_ = bf16[2,4,1,32,1792]{4,3,2,1,0:T(8,128)(2,1)S(1)} collective-permute-done((bf16[2,4,1,32,1792]{4,3,2,1,0:T(8,128)(2,1)}, bf16[2,4,1,32,1792]{4,3,2,1,0:T(8,128)(2,1)S(1)}, u32[]{:S(2)}, u32[]{:S(2)}) %collective-permute-start.76) | collective-permute-done | bytes 917536 | tf_op jit(solution)/shard_map/ppermute | solution.py:288
  491.5 12.3 %collective-permute-done.61.refs_0_.refs_4_ = bf16[2,4,1,32,1792]{4,3,2,1,0:T(8,128)(2,1)S(1)} collective-permute-done((bf16[2,4,1,32,1792]{4,3,2,1,0:T(8,128)(2,1)}, bf16[2,4,1,32,1792]{4,3,2,1,0:T(8,128)(2,1)S(1)}, u32[]{:S(2)}, u32[]{:S(2)}) %collective-permute-start.61) | collective-permute-done | bytes 917536 | tf_op jit(solution)/shard_map/ppermute | solution.py:288
  505.1 43.0 %collective-permute-done.62.refs_1_.refs_5_ = bf16[2,4,1,32,1792]{4,3,2,1,0:T(8,128)(2,1)} collective-permute-done((bf16[2,4,1,32,1792]{4,3,2,1,0:T(8,128)(2,1)}, bf16[2,4,1,32,1792]{4,3,2,1,0:T(8,128)(2,1)}, u32[]{:S(2)}, u32[]{:S(2)}) %collective-permute-start.62) | collective-permute-done | bytes 917536 | tf_op jit(solution)/shard_map/ppermute | solution.py:288
  553.8 20.1 %collective-permute-done.47.refs_0_.refs_4_ = bf16[2,4,1,32,1792]{4,3,2,1,0:T(8,128)(2,1)S(1)} collective-permute-done((bf16[2,4,1,32,1792]{4,3,2,1,0:T(8,128)(2,1)}, bf16[2,4,1,32,1792]{4,3,2,1,0:T(8,128)(2,1)S(1)}, u32[]{:S(2)}, u32[]{:S(2)}) %collective-permute-start.47) | collective-permute-done | bytes 917536 | tf_op jit(solution)/shard_map/ppermute | solution.py:288
  575.3 18.4 %collective-permute-done.48.refs_1_.refs_5_ = bf16[2,4,1,32,1792]{4,3,2,1,0:T(8,128)(2,1)S(1)} collective-permute-done((bf16[2,4,1,32,1792]{4,3,2,1,0:T(8,128)(2,1)}, bf16[2,4,1,32,1792]{4,3,2,1,0:T(8,128)(2,1)S(1)}, u32[]{:S(2)}, u32[]{:S(2)}) %collective-permute-start.48) | collective-permute-done | bytes 917536 | tf_op jit(solution)/shard_map/ppermute | solution.py:288
  600.1 13.2 %collective-permute-done.33.refs_0_.refs_4_ = bf16[2,4,1,32,1792]{4,3,2,1,0:T(8,128)(2,1)S(1)} collective-permute-done((bf16[2,4,1,32,1792]{4,3,2,1,0:T(8,128)(2,1)}, bf16[2,4,1,32,1792]{4,3,2,1,0:T(8,128)(2,1)S(1)}, u32[]{:S(2)}, u32[]{:S(2)}) %collective-permute-start.33) | collective-permute-done | bytes 917536 | tf_op jit(solution)/shard_map/ppermute | solution.py:288
  614.6 18.4 %collective-permute-done.34.refs_1_.refs_5_ = bf16[2,4,1,32,1792]{4,3,2,1,0:T(8,128)(2,1)S(1)} collective-permute-done((bf16[2,4,1,32,1792]{4,3,2,1,0:T(8,128)(2,1)}, bf16[2,4,1,32,1792]{4,3,2,1,0:T(8,128)(2,1)S(1)}, u32[]{:S(2)}, u32[]{:S(2)}) %collective-permute-start.34) | collective-permute-done | bytes 917536 | tf_op jit(solution)/shard_map/ppermute | solution.py:288
  640.6 12.1 %collective-permute-done.19.refs_0_.refs_4_ = bf16[2,4,1,32,1792]{4,3,2,1,0:T(8,128)(2,1)} collective-permute-done((bf16[2,4,1,32,1792]{4,3,2,1,0:T(8,128)(2,1)}, bf16[2,4,1,32,1792]{4,3,2,1,0:T(8,128)(2,1)}, u32[]{:S(2)}, u32[]{:S(2)}) %collective-permute-start.19) | collective-permute-done | bytes 917536 | tf_op jit(solution)/shard_map/ppermute | solution.py:288
  654.0 18.3 %collective-permute-done.20.refs_1_.refs_5_ = bf16[2,4,1,32,1792]{4,3,2,1,0:T(8,128)(2,1)S(1)} collective-permute-done((bf16[2,4,1,32,1792]{4,3,2,1,0:T(8,128)(2,1)}, bf16[2,4,1,32,1792]{4,3,2,1,0:T(8,128)(2,1)S(1)}, u32[]{:S(2)}, u32[]{:S(2)}) %collective-permute-start.20) | collective-permute-done | bytes 917536 | tf_op jit(solution)/shard_map/ppermute | solution.py:288
  697.5 14.1 %collective-permute-done.6.refs_1_.refs_5_ = bf16[2,4,1,32,1792]{4,3,2,1,0:T(8,128)(2,1)S(1)} collective-permute-done((bf16[2,4,1,32,1792]{4,3,2,1,0:T(8,128)(2,1)}, bf16[2,4,1,32,1792]{4,3,2,1,0:T(8,128)(2,1)S(1)}, u32[]{:S(2)}, u32[]{:S(2)}) %collective-permute-start.6) | collective-permute-done | bytes 917536 | tf_op jit(solution)/shard_map/ppermute | solution.py:288
  738.7 12.8 %collective-permute-done.65.refs_0_.refs_8_ = bf16[2,4,1,32,1792]{4,3,2,1,0:T(8,128)(2,1)S(1)} collective-permute-done((bf16[2,4,1,32,1792]{4,3,2,1,0:T(8,128)(2,1)S(1)}, bf16[2,4,1,32,1792]{4,3,2,1,0:T(8,128)(2,1)S(1)}, u32[]{:S(2)}, u32[]{:S(2)}) %collective-permute-start.65) | collective-permute-done | bytes 917536 | tf_op jit(solution)/shard_map/ppermute | solution.py:288
  759.1 12.1 %collective-permute-done.51.refs_0_.refs_8_ = bf16[2,4,1,32,1792]{4,3,2,1,0:T(8,128)(2,1)S(1)} collective-permute-done((bf16[2,4,1,32,1792]{4,3,2,1,0:T(8,128)(2,1)S(1)}, bf16[2,4,1,32,1792]{4,3,2,1,0:T(8,128)(2,1)S(1)}, u32[]{:S(2)}, u32[]{:S(2)}) %collective-permute-start.51) | collective-permute-done | bytes 917536 | tf_op jit(solution)/shard_map/ppermute | solution.py:288
  793.6 17.0 %collective-permute-done.23.refs_0_.refs_8_ = bf16[2,4,1,32,1792]{4,3,2,1,0:T(8,128)(2,1)} collective-permute-done((bf16[2,4,1,32,1792]{4,3,2,1,0:T(8,128)(2,1)}, bf16[2,4,1,32,1792]{4,3,2,1,0:T(8,128)(2,1)}, u32[]{:S(2)}, u32[]{:S(2)}) %collective-permute-start.23) | collective-permute-done | bytes 917536 | tf_op jit(solution)/shard_map/ppermute | solution.py:288
  813.4 16.8 %collective-permute-done.9.refs_0_.refs_8_ = bf16[2,4,1,32,1792]{4,3,2,1,0:T(8,128)(2,1)S(1)} collective-permute-done((bf16[2,4,1,32,1792]{4,3,2,1,0:T(8,128)(2,1)S(1)}, bf16[2,4,1,32,1792]{4,3,2,1,0:T(8,128)(2,1)S(1)}, u32[]{:S(2)}, u32[]{:S(2)}) %collective-permute-start.9) | collective-permute-done | bytes 917536 | tf_op jit(solution)/shard_map/ppermute | solution.py:288
  (436 shorter events, 436.4 us)
Async XLA Ops:
  69.2 106.6 %all-gather.4.cloned.1.call-start = ((), (), s32[]{:S(2)}) async-start(), calls=%async_computation.7 | async-start | bytes 2064384 | tf_op jit(solution)/shard_map/all_gather | solution.py:375
  121.3 263.0 %all-reduce.3.cloned.1.call-start = ((), (), s32[]{:S(2)}) async-start(), calls=%async_computation.9 | async-start | bytes 4194304
  212.1 107.0 %collective-permute-start.44 = (bf16[2,4,1,32,1792]{4,3,2,1,0:T(8,128)(2,1)}, bf16[2,4,1,32,1792]{4,3,2,1,0:T(8,128)(2,1)}, u32[]{:S(2)}, u32[]{:S(2)}) collective-permute-start(bf16[2,4,1,32,1792]{4,3,2,1,0:T(8,128)(2,1)} %get-tuple-element.67), channel_id=1, source_target_pairs={{6,4},{7,5},{4,2},{5,3},{2,0},{3,1},{14,12},{15,13},{12,10},{13,11... | collective-permute-start | bytes 2752520 | tf_op jit(solution)/shard_map/ppermute | solution.py:288
  231.7 89.3 %collective-permute-start.42 = (bf16[2,4,1,32,1792]{4,3,2,1,0:T(8,128)(2,1)}, bf16[2,4,1,32,1792]{4,3,2,1,0:T(8,128)(2,1)}, u32[]{:S(2)}, u32[]{:S(2)}) collective-permute-start(bf16[2,4,1,32,1792]{4,3,2,1,0:T(8,128)(2,1)} %get-tuple-element.65), channel_id=1, source_target_pairs={{0,2},{1,3},{2,4},{3,5},{4,6},{5,7},{8,10},{9,11},{10,12},{11,13},... | collective-permute-start | bytes 2752520 | tf_op jit(solution)/shard_map/ppermute | solution.py:288
  233.6 88.7 %collective-permute-start.43 = (bf16[2,4,1,32,1792]{4,3,2,1,0:T(8,128)(2,1)}, bf16[2,4,1,32,1792]{4,3,2,1,0:T(8,128)(2,1)}, u32[]{:S(2)}, u32[]{:S(2)}) collective-permute-start(bf16[2,4,1,32,1792]{4,3,2,1,0:T(8,128)(2,1)} %get-tuple-element.66), channel_id=1, source_target_pairs={{0,2},{1,3},{2,4},{3,5},{8,10},{9,11},{10,12},{11,13},{16,18},{17,... | collective-permute-start | bytes 2752520 | tf_op jit(solution)/shard_map/ppermute | solution.py:288
  237.5 88.8 %collective-permute-start.49 = (bf16[2,4,1,32,1792]{4,3,2,1,0:T(8,128)(2,1)}, bf16[2,4,1,32,1792]{4,3,2,1,0:T(8,128)(2,1)}, u32[]{:S(2)}, u32[]{:S(2)}) collective-permute-start(bf16[2,4,1,32,1792]{4,3,2,1,0:T(8,128)(2,1)} %get-tuple-element.68), channel_id=1, source_target_pairs={{6,4},{7,5},{4,2},{5,3},{14,12},{15,13},{12,10},{13,11},{22,20},{2... | collective-permute-start | bytes 2752520 | tf_op jit(solution)/shard_map/ppermute | solution.py:288
  251.3 77.0 %collective-permute-start.30 = (bf16[2,4,1,32,1792]{4,3,2,1,0:T(8,128)(2,1)}, bf16[2,4,1,32,1792]{4,3,2,1,0:T(8,128)(2,1)S(1)}, u32[]{:S(2)}, u32[]{:S(2)}) collective-permute-start(bf16[2,4,1,32,1792]{4,3,2,1,0:T(8,128)(2,1)} %get-tuple-element.61), channel_id=1, source_target_pairs={{6,4},{7,5},{4,2},{5,3},{2,0},{3,1},{14,12},{15,13},{12,10},{13,11... | collective-permute-start | bytes 2752520 | tf_op jit(solution)/shard_map/ppermute | solution.py:288
  255.5 79.3 %all-to-all-start = ((bf16[4,4,1,32,1792]{4,3,2,1,0:T(8,128)(2,1)}), bf16[4,4,1,32,1792]{4,3,2,1,0:T(8,128)(2,1)S(1)}, u32[]{:S(2)}, u32[]{:S(2)}) async-start(bf16[4,4,1,32,1792]{4,3,2,1,0:T(8,128)(2,1)} %copy-done.42), calls=%async_computation | async-start | bytes 3670016 | tf_op jit(solution)/shard_map/all_to_all | solution.py:369
  259.1 620.3 %reduce-scatter.2.cloned.1.call-start = ((), (), s32[]{:S(2)}) async-start(), calls=%async_computation.8 | async-start | bytes 4128768 | tf_op jit(solution)/shard_map/reduce_scatter | solution.py:401
  343.0 59.0 %collective-permute-start.15 = (bf16[2,4,1,32,1792]{4,3,2,1,0:T(8,128)(2,1)}, bf16[2,4,1,32,1792]{4,3,2,1,0:T(8,128)(2,1)}, u32[]{:S(2)}, u32[]{:S(2)}) collective-permute-start(bf16[2,4,1,32,1792]{4,3,2,1,0:T(8,128)(2,1)} %copy-done.80), channel_id=1, source_target_pairs={{0,2},{1,3},{2,4},{3,5},{8,10},{9,11},{10,12},{11,13},{16,18},{17,... | collective-permute-start | bytes 2752520 | tf_op jit(solution)/shard_map/ppermute | solution.py:288
  424.9 58.8 %collective-permute-start.78 = (bf16[2,4,1,32,1792]{4,3,2,1,0:T(8,128)(2,1)}, bf16[2,4,1,32,1792]{4,3,2,1,0:T(8,128)(2,1)S(1)}, u32[]{:S(2)}, u32[]{:S(2)}) collective-permute-start(bf16[2,4,1,32,1792]{4,3,2,1,0:T(8,128)(2,1)} %collective-permute-done.77.refs_2_.refs_10_), channel_id=1, source_target_pairs={{4,2},{5,3},{12,10},{13,11},{20,18},{21,19},{28,26},{29,27}} | collective-permute-start | bytes 2752520 | tf_op jit(solution)/shard_map/ppermute | solution.py:288
  444.1 59.7 %collective-permute-start.61 = (bf16[2,4,1,32,1792]{4,3,2,1,0:T(8,128)(2,1)}, bf16[2,4,1,32,1792]{4,3,2,1,0:T(8,128)(2,1)S(1)}, u32[]{:S(2)}, u32[]{:S(2)}) collective-permute-start(bf16[2,4,1,32,1792]{4,3,2,1,0:T(8,128)(2,1)} %collective-permute-done.56.refs_0_.refs_1_), channel_id=1, source_target_pairs={{2,4},{3,5},{4,6},{5,7},{10,12},{11,13},{12,14},{13,15},{18,20},{1... | collective-permute-start | bytes 2752520 | tf_op jit(solution)/shard_map/ppermute | solution.py:288
  461.8 86.2 %collective-permute-start.62 = (bf16[2,4,1,32,1792]{4,3,2,1,0:T(8,128)(2,1)}, bf16[2,4,1,32,1792]{4,3,2,1,0:T(8,128)(2,1)}, u32[]{:S(2)}, u32[]{:S(2)}) collective-permute-start(bf16[2,4,1,32,1792]{4,3,2,1,0:T(8,128)(2,1)} %collective-permute-done.57.refs_1_.refs_2_), channel_id=1, source_target_pairs={{2,4},{3,5},{10,12},{11,13},{18,20},{19,21},{26,28},{27,29}} | collective-permute-start | bytes 2752520 | tf_op jit(solution)/shard_map/ppermute | solution.py:288
  481.5 67.8 %collective-permute-start.64 = (bf16[2,4,1,32,1792]{4,3,2,1,0:T(8,128)(2,1)}, bf16[2,4,1,32,1792]{4,3,2,1,0:T(8,128)(2,1)}, u32[]{:S(2)}, u32[]{:S(2)}) collective-permute-start(bf16[2,4,1,32,1792]{4,3,2,1,0:T(8,128)(2,1)} %collective-permute-done.63.refs_2_.refs_10_), channel_id=1, source_target_pairs={{4,2},{5,3},{12,10},{13,11},{20,18},{21,19},{28,26},{29,27}} | collective-permute-start | bytes 2752520 | tf_op jit(solution)/shard_map/ppermute | solution.py:288
  484.7 67.2 %collective-permute-start.45 = (bf16[2,4,1,32,1792]{4,3,2,1,0:T(8,128)(2,1)}, bf16[2,4,1,32,1792]{4,3,2,1,0:T(8,128)(2,1)}, u32[]{:S(2)}, u32[]{:S(2)}) collective-permute-start(bf16[2,4,1,32,1792]{4,3,2,1,0:T(8,128)(2,1)} %collective-permute-done.44.refs_1_.refs_9_), channel_id=1, source_target_pairs={{4,2},{5,3},{2,0},{3,1},{12,10},{13,11},{10,8},{11,9},{20,18},{21,... | collective-permute-start | bytes 2752520 | tf_op jit(solution)/shard_map/ppermute | solution.py:288
  489.6 84.4 %collective-permute-start.47 = (bf16[2,4,1,32,1792]{4,3,2,1,0:T(8,128)(2,1)}, bf16[2,4,1,32,1792]{4,3,2,1,0:T(8,128)(2,1)S(1)}, u32[]{:S(2)}, u32[]{:S(2)}) collective-permute-start(bf16[2,4,1,32,1792]{4,3,2,1,0:T(8,128)(2,1)} %collective-permute-done.42.refs_0_.refs_1_), channel_id=1, source_target_pairs={{2,4},{3,5},{4,6},{5,7},{10,12},{11,13},{12,14},{13,15},{18,20},{1... | collective-permute-start | bytes 2752520 | tf_op jit(solution)/shard_map/ppermute | solution.py:288
  503.8 89.9 %collective-permute-start.48 = (bf16[2,4,1,32,1792]{4,3,2,1,0:T(8,128)(2,1)}, bf16[2,4,1,32,1792]{4,3,2,1,0:T(8,128)(2,1)S(1)}, u32[]{:S(2)}, u32[]{:S(2)}) collective-permute-start(bf16[2,4,1,32,1792]{4,3,2,1,0:T(8,128)(2,1)} %collective-permute-done.43.refs_1_.refs_2_), channel_id=1, source_target_pairs={{2,4},{3,5},{10,12},{11,13},{18,20},{19,21},{26,28},{27,29}} | collective-permute-start | bytes 2752520 | tf_op jit(solution)/shard_map/ppermute | solution.py:288
  551.9 61.4 %collective-permute-start.33 = (bf16[2,4,1,32,1792]{4,3,2,1,0:T(8,128)(2,1)}, bf16[2,4,1,32,1792]{4,3,2,1,0:T(8,128)(2,1)S(1)}, u32[]{:S(2)}, u32[]{:S(2)}) collective-permute-start(bf16[2,4,1,32,1792]{4,3,2,1,0:T(8,128)(2,1)} %collective-permute-done.28.refs_0_.refs_1_), channel_id=1, source_target_pairs={{2,4},{3,5},{4,6},{5,7},{10,12},{11,13},{12,14},{13,15},{18,20},{1... | collective-permute-start | bytes 2752520 | tf_op jit(solution)/shard_map/ppermute | solution.py:288
  574.0 59.0 %collective-permute-start.34 = (bf16[2,4,1,32,1792]{4,3,2,1,0:T(8,128)(2,1)}, bf16[2,4,1,32,1792]{4,3,2,1,0:T(8,128)(2,1)S(1)}, u32[]{:S(2)}, u32[]{:S(2)}) collective-permute-start(bf16[2,4,1,32,1792]{4,3,2,1,0:T(8,128)(2,1)} %collective-permute-done.29.refs_1_.refs_2_), channel_id=1, source_target_pairs={{2,4},{3,5},{10,12},{11,13},{18,20},{19,21},{26,28},{27,29}} | collective-permute-start | bytes 2752520 | tf_op jit(solution)/shard_map/ppermute | solution.py:288
  613.3 59.0 %collective-permute-start.20 = (bf16[2,4,1,32,1792]{4,3,2,1,0:T(8,128)(2,1)}, bf16[2,4,1,32,1792]{4,3,2,1,0:T(8,128)(2,1)S(1)}, u32[]{:S(2)}, u32[]{:S(2)}) collective-permute-start(bf16[2,4,1,32,1792]{4,3,2,1,0:T(8,128)(2,1)} %collective-permute-done.15.refs_1_.refs_2_), channel_id=1, source_target_pairs={{2,4},{3,5},{10,12},{11,13},{18,20},{19,21},{26,28},{27,29}} | collective-permute-start | bytes 2752520 | tf_op jit(solution)/shard_map/ppermute | solution.py:288
  652.7 58.9 %collective-permute-start.6 = (bf16[2,4,1,32,1792]{4,3,2,1,0:T(8,128)(2,1)}, bf16[2,4,1,32,1792]{4,3,2,1,0:T(8,128)(2,1)S(1)}, u32[]{:S(2)}, u32[]{:S(2)}) collective-permute-start(bf16[2,4,1,32,1792]{4,3,2,1,0:T(8,128)(2,1)} %copy-done.29), channel_id=1, source_target_pairs={{2,4},{3,5},{10,12},{11,13},{18,20},{19,21},{26,28},{27,29}} | collective-permute-start | bytes 2752520 | tf_op jit(solution)/shard_map/ppermute | solution.py:288
  733.6 57.3 %collective-permute-start.37 = (bf16[2,4,1,32,1792]{4,3,2,1,0:T(8,128)(2,1)S(1)}, bf16[2,4,1,32,1792]{4,3,2,1,0:T(8,128)(2,1)}, u32[]{:S(2)}, u32[]{:S(2)}) collective-permute-start(bf16[2,4,1,32,1792]{4,3,2,1,0:T(8,128)(2,1)S(1)} %collective-permute-done.33.refs_0_.refs_4_), channel_id=1, source_target_pairs={{4,6},{5,7},{12,14},{13,15},{20,22},{21,23},{28,30},{29,31}} | collective-permute-start | bytes 2752520 | tf_op jit(solution)/shard_map/ppermute | solution.py:288
  772.1 58.1 %collective-permute-start.9 = (bf16[2,4,1,32,1792]{4,3,2,1,0:T(8,128)(2,1)S(1)}, bf16[2,4,1,32,1792]{4,3,2,1,0:T(8,128)(2,1)S(1)}, u32[]{:S(2)}, u32[]{:S(2)}) collective-permute-start(bf16[2,4,1,32,1792]{4,3,2,1,0:T(8,128)(2,1)S(1)} %collective-permute-done.5.refs_0_.refs_4_), channel_id=1, source_target_pairs={{4,6},{5,7},{12,14},{13,15},{20,22},{21,23},{28,30},{29,31}} | collective-permute-start | bytes 2752520 | tf_op jit(solution)/shard_map/ppermute | solution.py:288
  776.3 62.4 %collective-permute-start.4 = (bf16[2,4,1,32,1792]{4,3,2,1,0:T(8,128)(2,1)S(1)}, bf16[2,4,1,32,1792]{4,3,2,1,0:T(8,128)(2,1)S(1)}, u32[]{:S(2)}, u32[]{:S(2)}) collective-permute-start(bf16[2,4,1,32,1792]{4,3,2,1,0:T(8,128)(2,1)S(1)} %collective-permute-done.3.refs_2_.refs_6_), channel_id=1, source_target_pairs={{2,0},{3,1},{10,8},{11,9},{18,16},{19,17},{26,24},{27,25}} | collective-permute-start | bytes 2752520 | tf_op jit(solution)/shard_map/ppermute | solution.py:288
  (163 other events, 4445.9 us)
Sparse Core Ops, SparseCore 0:
  72.2 29.0 all-gather.3
  208.6 84.2 all-reduce.2
  489.7 72.4 reduce-scatter.1

commit v3 on v0

v3 whole, which is shorter than its diff:
```python
import functools

import jax
import jax.numpy as jnp
from jax import lax
from jax.experimental import pallas as pl
from jax.experimental.pallas import tpu as pltpu
from jax.sharding import PartitionSpec as P

BLOCK = 128
CORES = 2
VMEM_BYTES = 48 * 1024 * 1024


def any_spec():
    return pl.BlockSpec(memory_space=pl.ANY)


def smem_spec():
    return pl.BlockSpec(memory_space=pltpu.SMEM)


def quantize_kernel(trains, x_ref, *refs):
    q_ref, d_ref = refs[-2:]
    rows = BLOCK // trains
    features = x_ref.shape[-1]
    for col in range(features // BLOCK):
        cols = slice(col * BLOCK, (col + 1) * BLOCK)
        block = x_ref[0, :, cols]
        peak = jnp.max(jnp.max(jnp.abs(block), axis=0, keepdims=True), axis=1, keepdims=True)
        scale = peak.astype(jnp.bfloat16).astype(jnp.float32)
        quant = (block * (1.0 / scale)).astype(jnp.bfloat16)
        q_ref[:, 0, 0, :, cols] = quant.reshape(trains, rows, BLOCK)
        d_ref[0, 0, :, cols] = (quant.astype(jnp.float32) * scale).astype(jnp.bfloat16)


def quantize(master, first, count, trains, after=()):
    experts, _, features = master.shape
    rows = BLOCK // trains
    return pl.pallas_call(
        functools.partial(quantize_kernel, trains),
        grid=(experts, count),
        in_specs=[pl.BlockSpec((1, BLOCK, features), lambda e, b: (e, first + b, 0))]
        + [any_spec()] * len(after),
        out_specs=[
            pl.BlockSpec((trains, 1, 1, rows, features), lambda e, b: (0, e, b, 0, 0)),
            pl.BlockSpec((1, 1, BLOCK, features), lambda e, b: (e, b, 0, 0)),
        ],
        out_shape=[
            jax.ShapeDtypeStruct((trains, experts, count, rows, features), jnp.bfloat16),
            jax.ShapeDtypeStruct((experts, count, BLOCK, features), jnp.bfloat16),
        ],
        compiler_params=pltpu.CompilerParams(vmem_limit_bytes=VMEM_BYTES),
        cost_estimate=pl.CostEstimate(
            flops=8 * experts * count * BLOCK * features,
            bytes_accessed=8 * experts * count * BLOCK * features,
            transcendentals=0,
        ),
        name="quantize",
    )(master, *after)


def start_choice(plan_ref, arrays, choice, target, sem):
    tests, array, (kind, n) = choice
    ref = arrays[array]
    if kind == "is":
        view = ref.at[n]
    elif kind == "at":
        view = ref.at[plan_ref[n]]
    else:
        view = ref.at[:, plan_ref[n]]
    hit = None
    for place, value in tests:
        test = plan_ref[place] == value
        hit = test if hit is None else hit & test

    def go():
        pltpu.make_async_copy(view, target, sem).start()

    if hit is None:
        go()
    else:
        pl.when(hit)(go)


def pack_kernel(pieces, n_in, plan_ref, *refs):
    arrays = refs[:n_in]
    out, held, sem_in, sem_out = refs[-4:]
    for n, choices in enumerate(pieces):
        for choice in choices:
            start_choice(plan_ref, arrays, choice, held.at[n], sem_in.at[n])
    for n in range(len(pieces)):
        pltpu.make_async_copy(held.at[n], held.at[n], sem_in.at[n]).wait()
        pltpu.make_async_copy(held.at[n], out.at[n], sem_out.at[n]).start()
    for n in range(len(pieces)):
        pltpu.make_async_copy(held.at[n], out.at[n], sem_out.at[n]).wait()


class Arrays:
    def __init__(self):
        self.items = []

    def add(self, array):
        for n, item in enumerate(self.items):
            if item is array:
                return n
        self.items.append(array)
        return len(self.items) - 1


def number_choices(pieces, arrays):
    return [[(tests, arrays.add(a), index) for tests, a, index in choices] for choices in pieces]


def pack(plan, shape, pieces, after=()):
    arrays = Arrays()
    pieces = number_choices(pieces, arrays)
    n_in = len(arrays.items)
    size = len(pieces)
    for dim in shape:
        size *= dim
    operands = arrays.items + list(after)
    return pl.pallas_call(
        functools.partial(pack_kernel, pieces, n_in),
        in_specs=[smem_spec()] + [any_spec()] * len(operands),
        out_specs=any_spec(),
        out_shape=jax.ShapeDtypeStruct((len(pieces),) + shape, jnp.bfloat16),
        scratch_shapes=[
            pltpu.VMEM((len(pieces),) + shape, jnp.bfloat16),
            pltpu.SemaphoreType.DMA((len(pieces),)),
            pltpu.SemaphoreType.DMA((len(pieces),)),
        ],
        compiler_params=pltpu.CompilerParams(vmem_limit_bytes=VMEM_BYTES),
        cost_estimate=pl.CostEstimate(flops=0, bytes_accessed=4 * size, transcendentals=0),
        name="pack",
    )(plan, *operands)


def place_kernel(pieces, sources, first, blocks, n_in, plan_ref, *refs):
    arrays = refs[:n_in]
    out, held, sem_in, sem_out = refs[-4:]
    trains, count, _, features = held.shape[1:]
    for n, choices in enumerate(pieces):
        for choice in choices:
            start_choice(plan_ref, arrays, choice, held.at[n], sem_in.at[n])
    stores = []
    for n in range(len(pieces)):
        pltpu.make_async_copy(held.at[n], held.at[n], sem_in.at[n]).wait()
        start = plan_ref[sources[n]] * blocks + first
        for part in range(trains):
            store = pltpu.make_async_copy(
                held.at[n, part],
                out.at[pl.ds(start, count), :, pl.ds(part * features, features)],
                sem_out.at[n, part],
            )
            store.start()
            stores.append(store)
    for store in stores:
        store.wait()


def place_pieces(plan, shape, owners, pieces, sources, first, blocks, out):
    trains, count, rows, features = shape
    arrays = Arrays()
    pieces = number_choices(pieces, arrays)
    n_in = len(arrays.items)
    operands = arrays.items + ([] if out is None else [out])
    return pl.pallas_call(
        functools.partial(place_kernel, pieces, sources, first, blocks, n_in),
        in_specs=[smem_spec()] + [any_spec()] * len(operands),
        out_specs=any_spec(),
        out_shape=jax.ShapeDtypeStruct((owners * blocks, rows, trains * features), jnp.bfloat16),
        scratch_shapes=[
            pltpu.VMEM((len(pieces),) + shape, jnp.bfloat16),
            pltpu.SemaphoreType.DMA((len(pieces),)),
            pltpu.SemaphoreType.DMA((len(pieces), trains)),
        ],
        input_output_aliases={} if out is None else {len(operands): 0},
        compiler_params=pltpu.CompilerParams(vmem_limit_bytes=VMEM_BYTES),
        cost_estimate=pl.CostEstimate(
            flops=0,
            bytes_accessed=4 * len(pieces) * trains * count * rows * features,
            transcendentals=0,
        ),
        name="place_pieces",
    )(plan, *operands)


def count_distinct(placement, experts, owners):
    expert_range = jnp.arange(experts, dtype=jnp.int32)
    half = owners // 2
    held = placement[None, :] == expert_range[:, None]
    sides = [jnp.any(held[:, :half], axis=1), jnp.any(held[:, half:], axis=1)]
    return jnp.maximum(*[jnp.sum(side.astype(jnp.int32)) for side in sides])


def make_plan(placement, experts, owners, cap):
    me = lax.axis_index("roll")
    chip, core = me // CORES, me % CORES
    side = chip // 2
    inner = ((chip == 1) | (chip == 2)).astype(jnp.int32)
    expert_range = jnp.arange(experts, dtype=jnp.int32)
    owner_range = jnp.arange(owners, dtype=jnp.int32)
    owner_side = owner_range // (owners // 2)

    def ranks(on_side):
        held = (placement[None, :] == expert_range[:, None]) & (owner_side == on_side)[None, :]
        need = jnp.any(held, axis=1).astype(jnp.int32)
        ahead = (need[None, :] > need[:, None]) | (
            (need[None, :] == need[:, None]) & (expert_range[None, :] < expert_range[:, None])
        )
        return jnp.sum(ahead.astype(jnp.int32), axis=1)

    here, there = ranks(side), ranks(1 - side)
    send = jnp.sum(
        jnp.where(there[:, None] == expert_range[None, :], expert_range[:, None], 0), axis=0
    )

    def expert_of(owner):
        return jnp.sum(jnp.where(owner_range == owner, placement, 0))

    def rank_of(table, expert):
        return jnp.sum(jnp.where(expert_range == expert, table, 0))

    outer = 3 * side
    own, mate = expert_of(me), expert_of(chip * CORES + 1 - core)
    out0, out1 = expert_of(outer * CORES), expert_of(outer * CORES + 1)
    chip_of = [chip, 1 + 4 * side - chip, 2 - side, 3 - 3 * side]
    entries = {
        "inner": inner,
        "core": core,
        "own": own,
        "mate": mate,
        "out0": out0,
        "out1": out1,
        "here_own": jnp.minimum(rank_of(here, own), cap - 1),
        "here_mate": jnp.minimum(rank_of(here, mate), cap - 1),
        "here_out0": jnp.minimum(rank_of(here, out0), cap - 1),
        "here_out1": jnp.minimum(rank_of(here, out1), cap - 1),
        "there_own": rank_of(there, own),
        "there_mate": rank_of(there, mate),
    }
    for n, source in enumerate(chip_of):
        entries[f"from_own{n}"] = source * CORES + core
        entries[f"from_mate{n}"] = source * CORES + 1 - core
    places = {name: experts + n for n, name in enumerate(entries)}
    for slot in range(experts):
        places[f"send{slot}"] = slot
    plan = jnp.concatenate((send, jnp.stack([v.astype(jnp.int32) for v in entries.values()])))
    return plan, places


def line_schedule(chunks, experts, cap):
    head = min(2, chunks)
    middle = [("own", c) for c in range(head)]
    middle += [("far", c) for c in range(chunks)]
    middle += [("own", c) for c in range(head, chunks)]
    inwards = [[("far", c, s) for s in range(cap)] for c in range(chunks)]
    rest = [("near", c, s) for c in range(chunks) for s in range(cap, experts)]
    inwards += [rest[i : i + cap] for i in range(0, len(rest), cap)]
    fresh = [("x", c, i) for c in range(chunks) for i in range(CORES)]
    relayed = [(n + 2, (kind, c, i)) for n, (kind, c) in enumerate(middle) for i in range(CORES)]
    outwards = []
    n = 0
    while fresh or relayed or n < max(len(middle), len(inwards)):
        now = []
        while relayed and relayed[0][0] <= n and len(now) < cap:
            now.append(relayed.pop(0)[1])
        while fresh and fresh[0][1] <= n and len(now) < cap:
            now.append(fresh.pop(0))
        outwards.append(now)
        n += 1
    return middle, inwards, outwards


def link_pairs(chip_pairs, swap_chips=()):
    pairs = []
    for core in range(CORES):
        for a, b in chip_pairs:
            pairs.append((a * CORES + core, b * CORES + core))
        for chip in swap_chips:
            pairs.append((chip * CORES + core, chip * CORES + 1 - core))
    return pairs


def line_exchange(masters, placement, trains, owners, cap):
    experts, hidden_rows, features = masters[0].shape
    blocks = hidden_rows // BLOCK
    shape = (trains, 1, BLOCK // trains, features)
    plan, places = make_plan(placement, experts, owners, cap)
    chunks = [(m, b) for m in range(3) for b in range(blocks)]
    middle, inwards, outwards = line_schedule(len(chunks), experts, cap)
    rounds = len(outwards)
    edge_pairs = link_pairs([(0, 1), (1, 0), (2, 3), (3, 2)])
    middle_pairs = link_pairs([(1, 2), (2, 1)], swap_chips=(0, 3))
    swap_pairs = link_pairs([], swap_chips=range(4))
    is_inner, is_outer = (places["inner"], 1), (places["inner"], 0)

    xs, dequant = {}, [[], [], []]
    got_edge, got_middle, where = {}, {}, {}
    sent_edge = {}

    def prepare(c, after):
        m, b = chunks[c]
        quant, restored = quantize(masters[m], b, 1, trains, after)
        dequant[m].append(restored)
        xs[c] = lax.all_to_all(quant, "train", split_axis=0, concat_axis=0, tiled=True)

    def arrived(c, who):
        own = who == "own"
        pieces = [[((), xs[c], ("expert", places[who]))]]
        near = []
        for slot in range(experts):
            key = ("far", c, slot) if slot < cap else ("near", c, slot)
            n, i = where[key]
            near.append(((is_inner, (places[f"there_{who}"], slot)), got_edge[n], ("is", i)))
        pieces.append(near)
        pieces.append([((is_inner,), got_middle["own", c], ("at", places[f"here_{who}"]))])
        pieces.append([((is_inner,), got_middle["far", c], ("at", places[f"here_{who}"]))])
        for position, kind in ((1, "x"), (2, "own"), (3, "far")):
            for core in range(CORES):
                n, i = where["out", kind, c, core if own else 1 - core]
                pieces[position].append(
                    ((is_outer, (places["core"], core)), got_edge[n], ("is", i))
                )
        return pieces

    outs = [None, None, None]
    done = set()

    def finish(c):
        m, b = chunks[c]
        swapped = lax.ppermute(pack(plan, shape, arrived(c, "mate")), "roll", swap_pairs)
        pieces = arrived(c, "own") + [[((), swapped, ("is", n))] for n in range(4)]
        sources = [places[f"from_own{n}"] for n in range(4)]
        sources += [places[f"from_mate{n}"] for n in range(4)]
        outs[m] = place_pieces(plan, shape, owners, pieces, sources, b, blocks, outs[m])

    ready_in = {}
    for n, pieces in enumerate(inwards):
        for piece in pieces:
            ready_in[piece[1]] = max(ready_in.get(piece[1], 0), n)
    for n, pieces in enumerate(outwards):
        for piece in pieces:
            ready_in[piece[1]] = max(ready_in.get(piece[1], 0), n)

    for n in range(rounds):
        if n < len(chunks) and n not in xs:
            prepare(n, (sent_edge[n - 2],) if n >= 2 else ())
        ins = inwards[n] if n < len(inwards) else []
        outs_now = outwards[n]
        width = max(len(ins), len(outs_now))
        pieces = []
        for i in range(width):
            choices = []
            if i < len(outs_now):
                kind, c, core = outs_now[i]
                where["out", kind, c, core] = (n, i)
                if kind == "x":
                    choices.append(((is_inner,), xs[c], ("expert", places[f"out{core}"])))
                else:
                    choices.append(
                        ((is_inner,), got_middle[kind, c], ("at", places[f"here_out{core}"]))
                    )
            else:
                choices.append(((is_inner,), xs[min(n, len(chunks) - 1)], ("expert", places["own"])))
            if i < len(ins):
                kind, c, slot = ins[i]
                where[kind, c, slot] = (n, i)
                choices.append(((is_outer,), xs[c], ("expert", places[f"send{slot}"])))
            else:
                choices.append(((is_outer,), xs[min(n, len(chunks) - 1)], ("expert", places["own"])))
            pieces.append(choices)
        if width:
            after = (got_edge[n - 2],) if n >= 2 else ()
            sent_edge[n] = pack(plan, shape, pieces, after)
            got_edge[n] = lax.ppermute(sent_edge[n], "roll", edge_pairs)
        if n < len(middle):
            kind, c = middle[n]
            if kind == "own":
                pieces = [[((), xs[c], ("expert", places[f"send{s}"]))] for s in range(cap)]
                after = (got_middle[middle[n - 2]],) if n >= 2 else ()
                going = pack(plan, shape, pieces, after)
            else:
                going = got_edge[where["far", c, 0][0]]
            got_middle[kind, c] = lax.ppermute(going, "roll", middle_pairs)
        for c in range(len(chunks)):
            if c in ready_in and ready_in[c] == n - 1:
                finish(c)
                done.add(c)
    for c in range(len(chunks)):
        if c not in done:
            finish(c)
    return outs, dequant


def direct_exchange(masters, placement, trains, owners):
    experts, hidden_rows, features = masters[0].shape
    blocks = hidden_rows // BLOCK
    rows = BLOCK // trains
    outs, dequant = [], []
    for master in masters:
        quant, restored = quantize(master, 0, blocks, trains)
        dequant.append([restored])
        x = lax.all_to_all(quant, "train", split_axis=0, concat_axis=0, tiled=True)
        x = jnp.transpose(x, (1, 2, 3, 0, 4)).reshape(experts, blocks, rows, trains * features)
        picked = jnp.take(x, placement, axis=0)
        got = lax.all_to_all(picked, "roll", split_axis=0, concat_axis=0, tiled=True)
        outs.append(got.reshape(owners * blocks, rows, trains * features))
    return outs, dequant


def select_experts(pre, onehot):
    tokens, top, experts = onehot.shape
    pre = pre.reshape(tokens, experts, -1)
    total = jnp.zeros((tokens, top, pre.shape[2]), jnp.float32)
    for expert in range(experts):
        total = total + jnp.where(onehot[:, :, expert, None], pre[:, None, expert], 0.0)
    return total


def gather_tokens(tokens, expert_ids, gate_weights, features):
    mine = lax.dynamic_slice_in_dim(tokens, lax.axis_index("train") * features, features, axis=1)
    top = expert_ids.shape[1]
    high = lax.reduce_precision(gate_weights, 8, 7)
    middle = lax.reduce_precision(gate_weights - high, 8, 7)
    low = gate_weights - high - middle
    beside = jnp.concatenate((expert_ids.astype(jnp.float32), high, middle, low), axis=1)
    beside = jnp.pad(beside, ((0, 0), (0, BLOCK - 4 * top))).astype(jnp.bfloat16)
    every = lax.all_gather(jnp.concatenate((mine, beside), axis=1), "roll", axis=0, tiled=True)
    side = every[:, features : features + 4 * top].astype(jnp.float32)
    ids = side[:, :top].astype(jnp.int32)
    weights = side[:, top : 2 * top] + side[:, 2 * top : 3 * top] + side[:, 3 * top :]
    return every[:, :features], ids, weights


def decode_step(tokens, ids, weights, dequant, experts):
    features = tokens.shape[1]
    onehot = ids[:, :, None] == jnp.arange(experts, dtype=jnp.int32)
    parts = []
    for m in range(2):
        for restored in dequant[m]:
            flat = restored.reshape(-1, features)
            pre = lax.dot_general(
                tokens, flat, (((1,), (1,)), ((), ())), preferred_element_type=jnp.float32
            )
            parts.append(select_experts(pre, onehot))
    pre = lax.psum(jnp.concatenate(parts, axis=2), "train")
    hidden_rows = pre.shape[2] // 2
    hidden = (jax.nn.silu(pre[:, :, :hidden_rows]) * pre[:, :, hidden_rows:]).astype(jnp.bfloat16)
    down = jnp.concatenate(dequant[2], axis=1) if len(dequant[2]) > 1 else dequant[2][0]
    mixed = jnp.zeros((tokens.shape[0], features), jnp.float32)
    for expert in range(experts):
        mask = onehot[:, :, expert]
        routed = jnp.sum(jnp.where(mask[:, :, None], hidden, jnp.zeros((), hidden.dtype)), axis=1)
        weight = jnp.sum(jnp.where(mask, weights, 0.0), axis=1)
        value = jnp.dot(
            routed, down[expert].reshape(hidden_rows, features), preferred_element_type=jnp.float32
        )
        mixed = mixed + weight[:, None] * value
    return lax.psum_scatter(mixed, "roll", scatter_dimension=0, tiled=True).astype(jnp.bfloat16)


def per_device(master_gate, master_up, master_down, tokens, expert_ids, gate_weights, placement):
    trains = lax.axis_size("train")
    owners = lax.axis_size("roll")
    experts, _, features = master_gate.shape
    masters = (master_gate, master_up, master_down)
    routed = gather_tokens(tokens, expert_ids, gate_weights, features)

    def run(exchange, masters, placement, routed):
        outs, dequant = exchange(masters, placement)
        return tuple(outs) + (decode_step(*routed, dequant, experts),)

    if owners // CORES == 4:
        most = min(experts, owners // 2)
        branches = []
        for cap in (most - 1, most):
            def exchange(masters, placement, cap=cap):
                return line_exchange(masters, placement, trains, owners, cap)

            branches.append(functools.partial(run, exchange))
        tight = count_distinct(placement, experts, owners) <= most - 1
        outs = lax.cond(tight, branches[0], branches[1], masters, placement, routed)
    else:
        def exchange(masters, placement):
            return direct_exchange(masters, placement, trains, owners)

        outs = run(exchange, masters, placement, routed)
    return tuple(out[None] for out in outs[:3]) + (outs[3],)


def solution(mesh):
    in_specs = (
        P(None, "roll", "train"),
        P(None, "roll", "train"),
        P(None, "roll", "train"),
        P("roll", None),
        P("roll", None),
        P("roll", None),
        P(),
    )
    out_specs = (
        P("roll", None, "train", None),
        P("roll", None, "train", None),
        P("roll", None, "train", None),
        P("roll", "train"),
    )
    return jax.shard_map(
        per_device, mesh=mesh, in_specs=in_specs, out_specs=out_specs, check_vma=False
    )
```

time: 1150 us -> 630 us (0.55)
  blocking collectives: 329 us -> 0 us
  local copies, waits for them, and re-layouts: 259 us -> 53 us
  Pallas kernels: 0 us -> 109 us
  other arithmetic: 96.2 us -> 21.4 us
  waiting for transfers between devices: 376 us -> 336 us
    all_to_all x2 -> x0, blocking collectives: 329 us -> none  [the longest x1 165 us: per_device(): lax.all_to_all(picked_gate, 'roll', split_axis=0, concat_axis=0, tiled=True)]
    all_to_all x8 -> x6, waiting for transfers between devices: 327 us -> 26.6 us  [prepare(): lax.all_to_all(quant, 'train', split_axis=0, concat_axis=0, tiled=True)]
    ppermute x0 -> x32, waiting for transfers between devices: none -> 233 us  [the longest x12 122 us: line_exchange(): got_middle[kind, c] = lax.ppermute(going, 'roll', middle_pairs)]
    pallas_call x0 -> x38, Pallas kernels: none -> 109 us  [the longest x26 64.6 us: pack(): pl.pallas_call(functools.partial(pack_kernel, pieces, n_in), in_specs=[sm...]
    all_to_all x9 -> x0, local copies, waits for them, and re-layouts: 51.8 us -> none  [the longest x2 17.2 us: per_device(): lax.all_to_all(got_gate.reshape(flat_shape), 'train', split_axis=1, conca...]
    convert_element_type x11 -> x0, local copies, waits for them, and re-layouts: 50.9 us -> none  [the longest x4 38.7 us: dequantize_slot(): quantized.astype(jnp.float32)]
    reduce_scatter x1, waiting for transfers between devices: 49 us -> 0.02 us  [decode_step(): lax.psum_scatter(mixed, 'roll', scatter_dimension=0, tiled=True)]
    psum x0 -> x1, waiting for transfers between devices: none -> 48.7 us  [decode_step(): pre = lax.psum(jnp.concatenate(parts, axis=2), 'train')]
  transfers between devices with their start and end apart: 9 -> 41, of which waited for: 5 -> 17; matrix products, arithmetic and copies ran while one was open for 22% -> 11% of each run, Pallas kernels for 0% -> 17%
where the time goes in v3:
time: 630 us; the launch traced here: 618 us
  waiting for transfers between devices  336 us (53%)
  Pallas kernels  109 us (17%)
  local copies, waits for them, and re-layouts  53 us (8%)
  starting transfers between devices  49.3 us (8%)
  matrix products  22.7 us (4%)
  other arithmetic  21.4 us (3%)
  between operations  15.6 us (2%)
  loops' own time  11.2 us (2%)
    ppermute x12, waiting for transfers between devices, line_exchange(): got_middle[kind, c] = lax.ppermute(going, 'roll', middle_pairs)  122 us
    ppermute x14, waiting for transfers between devices, line_exchange(): got_edge[n] = lax.ppermute(sent_edge[n], 'roll', edge_pairs)  111 us
    pallas_call x26, Pallas kernels, pack(): pl.pallas_call(functools.partial(pack_kernel, pieces, n_in), in_specs=[sm...  64.6 us
    psum x1, waiting for transfers between devices, decode_step(): pre = lax.psum(jnp.concatenate(parts, axis=2), 'train')  48.7 us
    all_gather x1, waiting for transfers between devices, gather_tokens(): lax.all_gather(jnp.concatenate((mine, beside), axis=1), 'roll', axis=0, t...  26.9 us
    all_to_all x6, waiting for transfers between devices, prepare(): lax.all_to_all(quant, 'train', split_axis=0, concat_axis=0, tiled=True)  26.6 us
    unnamed x116, local copies, waits for them, and re-layouts  24.8 us
    all_to_all x6, starting transfers between devices, prepare(): lax.all_to_all(quant, 'train', split_axis=0, concat_axis=0, tiled=True)  23.7 us
  transfers between devices with their start and end apart: 41, of which 17 were waited for; matrix products, arithmetic and copies ran while one was open for 11% of the time, Pallas kernels for 17%

profile of v3, /device:TPU:19, one launch (start us, length us, event | category | flops | bytes accessed | tf_op | source)
XLA Modules:
  0.0 617.8 jit_solution(13223751164437631209)
XLA Ops:
  12.4 26.9 %all-gather.2.cloned.1.call-done = bf16[512,1920]{1,0:T(8,128)(2,1)} async-done(((bf16[64,1920]{1,0:T(8,128)(2,1)}), bf16[512,1920]{1,0:T(8,128)(2,1)}) %all-gather.2.cloned.1.call-update) | async-done | bytes 1966096 | tf_op jit(solution)/shard_map/all_gather | solution.py:430
  40.2 568.7 %conditional.4 = (bf16[1,16,32,7168]{3,2,1,0:T(8,128)(2,1)}, bf16[1,16,32,7168]{3,2,1,0:T(8,128)(2,1)}, bf16[1,16,32,7168]{3,2,1,0:T(8,128)(2,1)}, f32[64,1792]{1,0:T(8,128)}) conditional(s32[]{:T(128)} %convert_element_type.111, (s32[8]{0:T(128)S(1)}, f32[4,256,1792]{2,1,0:T(8,128)}, f32[4,256,1792]{2,1,0:T(8,128)}, f32[4,256,1792]{2,1,0:T(8,128)}, ...), branch_computations={%region_4.30_spmd, %region_30.56_spmd} | conditional | flops 5696533504 | bytes 816422272
  63.7 15.2 %all-to-all-done.7.refs_0_.refs_1_ = bf16[4,4,1,32,1792]{4,3,2,1,0:T(8,128)(2,1)S(1)} async-done(((bf16[4,4,1,32,1792]{4,3,2,1,0:T(8,128)(2,1)}), bf16[4,4,1,32,1792]{4,3,2,1,0:T(8,128)(2,1)S(1)}, u32[]{:S(2)}, u32[]{:S(2)}) %all-to-all-start.7) | async-done | bytes 1835040 | tf_op jit(solution)/shard_map/cond/branch_1_fun/all_to_all | solution.py:307
  93.1 3.9 concatenate.20.plan_ref
  176.8 4.6 all-to-all-start.9
  195.3 11.4 %all-to-all-done.9.refs_1_.refs_3_.refs_2_.refs_0_ = bf16[4,4,1,32,1792]{4,3,2,1,0:T(8,128)(2,1)} async-done(((bf16[4,4,1,32,1792]{4,3,2,1,0:T(8,128)(2,1)}), bf16[4,4,1,32,1792]{4,3,2,1,0:T(8,128)(2,1)}, u32[]{:S(2)}, u32[]{:S(2)}) %all-to-all-start.9) | async-done | bytes 1835040 | tf_op jit(solution)/shard_map/cond/branch_1_fun/all_to_all | solution.py:307
  206.8 4.2 all-to-all-start.11
  211.2 4.0 fusion.66
  215.2 48.7 %all-reduce.6.cloned.1.call-done = f32[512,2,512]{2,0,1:T(8,128)} async-done(((f32[512,2,512]{2,0,1:T(8,128)}), f32[512,2,512]{2,0,1:T(8,128)}) %all-reduce.6.cloned.1.call-update) | async-done | bytes 2097168 | tf_op jit(solution)/shard_map/cond/branch_1_fun/psum | solution.py:448
  283.9 4.4 multiply_add_fusion.1
  288.3 27.1 %collective-permute-done.38.refs_5_.refs_6_.refs_4_.refs_3_.refs_1_ = bf16[3,4,1,32,1792]{4,3,2,1,0:T(8,128)(2,1)} collective-permute-done((bf16[3,4,1,32,1792]{4,3,2,1,0:T(8,128)(2,1)}, bf16[3,4,1,32,1792]{4,3,2,1,0:T(8,128)(2,1)}, u32[]{:S(2)}, u32[]{:S(2)}) %collective-permute-start.38) | collective-permute-done | bytes 1376288 | tf_op jit(solution)/shard_map/cond/branch_1_fun/ppermute | solution.py:377
  316.8 53.2 %collective-permute-done.43.refs_6_.refs_4_.refs_3_.refs_1_ = bf16[3,4,1,32,1792]{4,3,2,1,0:T(8,128)(2,1)S(1)} collective-permute-done((bf16[3,4,1,32,1792]{4,3,2,1,0:T(8,128)(2,1)}, bf16[3,4,1,32,1792]{4,3,2,1,0:T(8,128)(2,1)S(1)}, u32[]{:S(2)}, u32[]{:S(2)}) %collective-permute-start.43) | collective-permute-done | bytes 1376288 | tf_op jit(solution)/shard_map/cond/branch_1_fun/ppermute | solution.py:377
  380.3 26.5 %collective-permute-done.53.refs_1_.refs_0_.refs_6_ = bf16[3,4,1,32,1792]{4,3,2,1,0:T(8,128)(2,1)S(1)} collective-permute-done((bf16[3,4,1,32,1792]{4,3,2,1,0:T(8,128)(2,1)}, bf16[3,4,1,32,1792]{4,3,2,1,0:T(8,128)(2,1)S(1)}, u32[]{:S(2)}, u32[]{:S(2)}) %collective-permute-start.53) | collective-permute-done | bytes 1376288 | tf_op jit(solution)/shard_map/cond/branch_1_fun/ppermute | solution.py:386
  410.2 26.2 %collective-permute-done.48.refs_1_.refs_0_.refs_7_ = bf16[3,4,1,32,1792]{4,3,2,1,0:T(8,128)(2,1)} collective-permute-done((bf16[3,4,1,32,1792]{4,3,2,1,0:T(8,128)(2,1)S(1)}, bf16[3,4,1,32,1792]{4,3,2,1,0:T(8,128)(2,1)}, u32[]{:S(2)}, u32[]{:S(2)}) %collective-permute-start.48) | collective-permute-done | bytes 1376288 | tf_op jit(solution)/shard_map/cond/branch_1_fun/ppermute | solution.py:386
  444.6 21.3 %collective-permute-done.54.refs_0_.refs_4_.refs_1_ = bf16[3,4,1,32,1792]{4,3,2,1,0:T(8,128)(2,1)} collective-permute-done((bf16[3,4,1,32,1792]{4,3,2,1,0:T(8,128)(2,1)}, bf16[3,4,1,32,1792]{4,3,2,1,0:T(8,128)(2,1)}, u32[]{:S(2)}, u32[]{:S(2)}) %collective-permute-start.54) | collective-permute-done | bytes 1376288 | tf_op jit(solution)/shard_map/cond/branch_1_fun/ppermute | solution.py:386
  469.0 26.2 %collective-permute-done.49.refs_0_.refs_5_.refs_1_ = bf16[3,4,1,32,1792]{4,3,2,1,0:T(8,128)(2,1)S(1)} collective-permute-done((bf16[3,4,1,32,1792]{4,3,2,1,0:T(8,128)(2,1)}, bf16[3,4,1,32,1792]{4,3,2,1,0:T(8,128)(2,1)S(1)}, u32[]{:S(2)}, u32[]{:S(2)}) %collective-permute-start.49) | collective-permute-done | bytes 1376288 | tf_op jit(solution)/shard_map/cond/branch_1_fun/ppermute | solution.py:386
  509.2 10.5 %collective-permute-done.56.refs_5_.refs_2_ = bf16[2,4,1,32,1792]{4,3,2,1,0:T(8,128)(2,1)S(1)} collective-permute-done((bf16[2,4,1,32,1792]{4,3,2,1,0:T(8,128)(2,1)S(1)}, bf16[2,4,1,32,1792]{4,3,2,1,0:T(8,128)(2,1)S(1)}, u32[]{:S(2)}, u32[]{:S(2)}) %collective-permute-start.56) | collective-permute-done | bytes 917536 | tf_op jit(solution)/shard_map/cond/branch_1_fun/ppermute | solution.py:377
  519.7 5.1 collective-permute-done.61.refs_0_.refs_4_
  527.5 11.9 %collective-permute-done.51.refs_6_.refs_2_ = bf16[2,4,1,32,1792]{4,3,2,1,0:T(8,128)(2,1)S(1)} collective-permute-done((bf16[2,4,1,32,1792]{4,3,2,1,0:T(8,128)(2,1)S(1)}, bf16[2,4,1,32,1792]{4,3,2,1,0:T(8,128)(2,1)S(1)}, u32[]{:S(2)}, u32[]{:S(2)}) %collective-permute-start.51) | collective-permute-done | bytes 917536 | tf_op jit(solution)/shard_map/cond/branch_1_fun/ppermute | solution.py:377
  539.4 15.0 %collective-permute-done.58.refs_0_.refs_5_ = bf16[3,4,1,32,1792]{4,3,2,1,0:T(8,128)(2,1)} collective-permute-done((bf16[3,4,1,32,1792]{4,3,2,1,0:T(8,128)(2,1)}, bf16[3,4,1,32,1792]{4,3,2,1,0:T(8,128)(2,1)}, u32[]{:S(2)}, u32[]{:S(2)}) %collective-permute-start.58) | collective-permute-done | bytes 1376288 | tf_op jit(solution)/shard_map/cond/branch_1_fun/ppermute | solution.py:386
  570.8 8.3 %collective-permute-done.59.refs_6_ = bf16[2,4,1,32,1792]{4,3,2,1,0:T(8,128)(2,1)S(1)} collective-permute-done((bf16[2,4,1,32,1792]{4,3,2,1,0:T(8,128)(2,1)S(1)}, bf16[2,4,1,32,1792]{4,3,2,1,0:T(8,128)(2,1)S(1)}, u32[]{:S(2)}, u32[]{:S(2)}) %collective-permute-start.59) | collective-permute-done | bytes 917536 | tf_op jit(solution)/shard_map/cond/branch_1_fun/ppermute | solution.py:377
  596.5 4.0 place_pieces.21
  600.6 4.1 place_pieces.22.refs_9_
  604.6 4.0 place_pieces.23
  (271 shorter events, 224.6 us)
Async XLA Ops:
  119.7 46.8 %collective-permute-start.34 = (bf16[3,4,1,32,1792]{4,3,2,1,0:T(8,128)(2,1)}, bf16[3,4,1,32,1792]{4,3,2,1,0:T(8,128)(2,1)}, u32[]{:S(2)}, u32[]{:S(2)}) collective-permute-start(bf16[3,4,1,32,1792]{4,3,2,1,0:T(8,128)(2,1)} %pack.80.refs_0_), channel_id=1, source_target_pairs={{0,2},{2,0},{4,6},{6,4},{1,3},{3,1},{5,7},{7,5},{8,10},{10,8},{12,... | collective-permute-start | bytes 4128776 | tf_op jit(solution)/shard_map/cond/branch_1_fun/ppermute | solution.py:377
  122.0 60.7 %collective-permute-start.32 = (bf16[3,4,1,32,1792]{4,3,2,1,0:T(8,128)(2,1)}, bf16[3,4,1,32,1792]{4,3,2,1,0:T(8,128)(2,1)}, u32[]{:S(2)}, u32[]{:S(2)}) collective-permute-start(bf16[3,4,1,32,1792]{4,3,2,1,0:T(8,128)(2,1)} %pack.78.refs_0_), channel_id=1, source_target_pairs={{0,2},{2,0},{4,6},{6,4},{1,3},{3,1},{5,7},{7,5},{8,10},{10,8},{12,... | collective-permute-start | bytes 4128776 | tf_op jit(solution)/shard_map/cond/branch_1_fun/ppermute | solution.py:377
  128.0 56.1 %collective-permute-start.40 = (bf16[3,4,1,32,1792]{4,3,2,1,0:T(8,128)(2,1)}, bf16[3,4,1,32,1792]{4,3,2,1,0:T(8,128)(2,1)}, u32[]{:S(2)}, u32[]{:S(2)}) collective-permute-start(bf16[3,4,1,32,1792]{4,3,2,1,0:T(8,128)(2,1)} %pack.84), channel_id=1, source_target_pairs={{2,4},{4,2},{0,1},{6,7},{3,5},{5,3},{1,0},{7,6},{10,12},{12,10},{8... | collective-permute-start | bytes 4128776 | tf_op jit(solution)/shard_map/cond/branch_1_fun/ppermute | solution.py:386
  142.0 121.9 %all-reduce.6.cloned.1.call-start = ((), (), s32[]{:S(2)}) async-start(), calls=%async_computation.16 | async-start | bytes 4194304 | tf_op jit(solution)/shard_map/cond/branch_1_fun/psum | solution.py:448
  181.8 90.1 %collective-permute-start.35 = (bf16[3,4,1,32,1792]{4,3,2,1,0:T(8,128)(2,1)}, bf16[3,4,1,32,1792]{4,3,2,1,0:T(8,128)(2,1)}, u32[]{:S(2)}, u32[]{:S(2)}) collective-permute-start(bf16[3,4,1,32,1792]{4,3,2,1,0:T(8,128)(2,1)} %pack.81.refs_0_), channel_id=1, source_target_pairs={{0,2},{2,0},{4,6},{6,4},{1,3},{3,1},{5,7},{7,5},{8,10},{10,8},{12,... | collective-permute-start | bytes 4128776 | tf_op jit(solution)/shard_map/cond/branch_1_fun/ppermute | solution.py:377
  187.0 88.8 %collective-permute-start.41 = (bf16[3,4,1,32,1792]{4,3,2,1,0:T(8,128)(2,1)}, bf16[3,4,1,32,1792]{4,3,2,1,0:T(8,128)(2,1)S(1)}, u32[]{:S(2)}, u32[]{:S(2)}) collective-permute-start(bf16[3,4,1,32,1792]{4,3,2,1,0:T(8,128)(2,1)} %pack.85.refs_0_), channel_id=1, source_target_pairs={{0,2},{2,0},{4,6},{6,4},{1,3},{3,1},{5,7},{7,5},{8,10},{10,8},{12,... | collective-permute-start | bytes 4128776 | tf_op jit(solution)/shard_map/cond/branch_1_fun/ppermute | solution.py:377
  187.1 84.7 %collective-permute-start.37 = (bf16[3,4,1,32,1792]{4,3,2,1,0:T(8,128)(2,1)}, bf16[3,4,1,32,1792]{4,3,2,1,0:T(8,128)(2,1)}, u32[]{:S(2)}, u32[]{:S(2)}) collective-permute-start(bf16[3,4,1,32,1792]{4,3,2,1,0:T(8,128)(2,1)} %collective-permute-done.34.refs_2_.refs_1_), channel_id=1, source_target_pairs={{2,4},{4,2},{0,1},{6,7},{3,5},{5,3},{1,0},{7,6},{10,12},{12,10},{8... | collective-permute-start | bytes 4128776 | tf_op jit(solution)/shard_map/cond/branch_1_fun/ppermute | solution.py:386
  188.0 87.8 %collective-permute-start.42 = (bf16[3,4,1,32,1792]{4,3,2,1,0:T(8,128)(2,1)}, bf16[3,4,1,32,1792]{4,3,2,1,0:T(8,128)(2,1)}, u32[]{:S(2)}, u32[]{:S(2)}) collective-permute-start(bf16[3,4,1,32,1792]{4,3,2,1,0:T(8,128)(2,1)} %collective-permute-done.32.refs_3_.refs_1_), channel_id=1, source_target_pairs={{2,4},{4,2},{0,1},{6,7},{3,5},{5,3},{1,0},{7,6},{10,12},{12,10},{8... | collective-permute-start | bytes 4128776 | tf_op jit(solution)/shard_map/cond/branch_1_fun/ppermute | solution.py:386
  206.8 69.0 %all-to-all-start.11 = ((bf16[4,4,1,32,1792]{4,3,2,1,0:T(8,128)(2,1)}), bf16[4,4,1,32,1792]{4,3,2,1,0:T(8,128)(2,1)S(1)}, u32[]{:S(2)}, u32[]{:S(2)}) async-start(bf16[4,4,1,32,1792]{4,3,2,1,0:T(8,128)(2,1)} %copy-done.55), calls=%async_computation.12 | async-start | bytes 3670016 | tf_op jit(solution)/shard_map/cond/branch_1_fun/all_to_all | solution.py:307
  211.0 397.7 %reduce-scatter.5.cloned.1.call-start = ((), (), s32[]{:S(2)}) async-start(), calls=%async_computation.17 | async-start | bytes 4128768 | tf_op jit(solution)/shard_map/cond/branch_1_fun/reduce_scatter | solution.py:461
  280.6 89.4 %collective-permute-start.43 = (bf16[3,4,1,32,1792]{4,3,2,1,0:T(8,128)(2,1)}, bf16[3,4,1,32,1792]{4,3,2,1,0:T(8,128)(2,1)S(1)}, u32[]{:S(2)}, u32[]{:S(2)}) collective-permute-start(bf16[3,4,1,32,1792]{4,3,2,1,0:T(8,128)(2,1)} %pack.86), channel_id=1, source_target_pairs={{0,2},{2,0},{4,6},{6,4},{1,3},{3,1},{5,7},{7,5},{8,10},{10,8},{12,... | collective-permute-start | bytes 4128776 | tf_op jit(solution)/shard_map/cond/branch_1_fun/ppermute | solution.py:377
  282.4 88.0 %collective-permute-start.36 = (bf16[3,4,1,32,1792]{4,3,2,1,0:T(8,128)(2,1)}, bf16[3,4,1,32,1792]{4,3,2,1,0:T(8,128)(2,1)}, u32[]{:S(2)}, u32[]{:S(2)}) collective-permute-start(bf16[3,4,1,32,1792]{4,3,2,1,0:T(8,128)(2,1)} %collective-permute-done.35.refs_3_.refs_4_.refs_1_), channel_id=1, source_target_pairs={{2,4},{4,2},{0,1},{6,7},{3,5},{5,3},{1,0},{7,6},{10,12},{12,10},{8... | collective-permute-start | bytes 4128776 | tf_op jit(solution)/shard_map/cond/branch_1_fun/ppermute | solution.py:386
  282.5 94.9 %collective-permute-start.46 = (bf16[3,4,1,32,1792]{4,3,2,1,0:T(8,128)(2,1)S(1)}, bf16[3,4,1,32,1792]{4,3,2,1,0:T(8,128)(2,1)}, u32[]{:S(2)}, u32[]{:S(2)}) collective-permute-start(bf16[3,4,1,32,1792]{4,3,2,1,0:T(8,128)(2,1)S(1)} %copy-done.13), channel_id=1, source_target_pairs={{2,4},{4,2},{0,1},{6,7},{3,5},{5,3},{1,0},{7,6},{10,12},{12,10},{8... | collective-permute-start | bytes 4128776 | tf_op jit(solution)/shard_map/cond/branch_1_fun/ppermute | solution.py:386
  315.4 91.4 %collective-permute-start.53 = (bf16[3,4,1,32,1792]{4,3,2,1,0:T(8,128)(2,1)}, bf16[3,4,1,32,1792]{4,3,2,1,0:T(8,128)(2,1)S(1)}, u32[]{:S(2)}, u32[]{:S(2)}) collective-permute-start(bf16[3,4,1,32,1792]{4,3,2,1,0:T(8,128)(2,1)} %collective-permute-done.38.refs_5_.refs_6_.refs_4_.refs_3_.refs_1_), channel_id=1, source_target_pairs={{2,4},{4,2},{0,1},{6,7},{3,5},{5,3},{1,0},{7,6},{10,12},{12,10},{8... | collective-permute-start | bytes 4128776 | tf_op jit(solution)/shard_map/cond/branch_1_fun/ppermute | solution.py:386
  370.0 66.4 %collective-permute-start.48 = (bf16[3,4,1,32,1792]{4,3,2,1,0:T(8,128)(2,1)S(1)}, bf16[3,4,1,32,1792]{4,3,2,1,0:T(8,128)(2,1)}, u32[]{:S(2)}, u32[]{:S(2)}) collective-permute-start(bf16[3,4,1,32,1792]{4,3,2,1,0:T(8,128)(2,1)S(1)} %collective-permute-done.43.refs_6_.refs_4_.refs_3_.refs_1_), channel_id=1, source_target_pairs={{2,4},{4,2},{0,1},{6,7},{3,5},{5,3},{1,0},{7,6},{10,12},{12,10},{8... | collective-permute-start | bytes 4128776 | tf_op jit(solution)/shard_map/cond/branch_1_fun/ppermute | solution.py:386
  374.9 63.8 %collective-permute-start.39 = (bf16[3,4,1,32,1792]{4,3,2,1,0:T(8,128)(2,1)}, bf16[3,4,1,32,1792]{4,3,2,1,0:T(8,128)(2,1)S(1)}, u32[]{:S(2)}, u32[]{:S(2)}) collective-permute-start(bf16[3,4,1,32,1792]{4,3,2,1,0:T(8,128)(2,1)} %pack.83), channel_id=1, source_target_pairs={{0,2},{2,0},{4,6},{6,4},{1,3},{3,1},{5,7},{7,5},{8,10},{10,8},{12,... | collective-permute-start | bytes 4128776 | tf_op jit(solution)/shard_map/cond/branch_1_fun/ppermute | solution.py:377
  380.3 60.9 %collective-permute-start.47 = (bf16[3,4,1,32,1792]{4,3,2,1,0:T(8,128)(2,1)}, bf16[3,4,1,32,1792]{4,3,2,1,0:T(8,128)(2,1)S(1)}, u32[]{:S(2)}, u32[]{:S(2)}) collective-permute-start(bf16[3,4,1,32,1792]{4,3,2,1,0:T(8,128)(2,1)} %pack.89), channel_id=1, source_target_pairs={{0,2},{2,0},{4,6},{6,4},{1,3},{3,1},{5,7},{7,5},{8,10},{10,8},{12,... | collective-permute-start | bytes 4128776 | tf_op jit(solution)/shard_map/cond/branch_1_fun/ppermute | solution.py:377
  409.8 56.1 %collective-permute-start.54 = (bf16[3,4,1,32,1792]{4,3,2,1,0:T(8,128)(2,1)}, bf16[3,4,1,32,1792]{4,3,2,1,0:T(8,128)(2,1)}, u32[]{:S(2)}, u32[]{:S(2)}) collective-permute-start(bf16[3,4,1,32,1792]{4,3,2,1,0:T(8,128)(2,1)} %pack.94), channel_id=1, source_target_pairs={{2,4},{4,2},{0,1},{6,7},{3,5},{5,3},{1,0},{7,6},{10,12},{12,10},{8... | collective-permute-start | bytes 4128776 | tf_op jit(solution)/shard_map/cond/branch_1_fun/ppermute | solution.py:386
  438.3 57.0 %collective-permute-start.49 = (bf16[3,4,1,32,1792]{4,3,2,1,0:T(8,128)(2,1)}, bf16[3,4,1,32,1792]{4,3,2,1,0:T(8,128)(2,1)S(1)}, u32[]{:S(2)}, u32[]{:S(2)}) collective-permute-start(bf16[3,4,1,32,1792]{4,3,2,1,0:T(8,128)(2,1)} %pack.90), channel_id=1, source_target_pairs={{2,4},{4,2},{0,1},{6,7},{3,5},{5,3},{1,0},{7,6},{10,12},{12,10},{8... | collective-permute-start | bytes 4128776 | tf_op jit(solution)/shard_map/cond/branch_1_fun/ppermute | solution.py:386
  441.1 56.5 %collective-permute-start.55 = (bf16[3,4,1,32,1792]{4,3,2,1,0:T(8,128)(2,1)}, bf16[3,4,1,32,1792]{4,3,2,1,0:T(8,128)(2,1)S(1)}, u32[]{:S(2)}, u32[]{:S(2)}) collective-permute-start(bf16[3,4,1,32,1792]{4,3,2,1,0:T(8,128)(2,1)} %pack.95), channel_id=1, source_target_pairs={{0,2},{2,0},{4,6},{6,4},{1,3},{3,1},{5,7},{7,5},{8,10},{10,8},{12,... | collective-permute-start | bytes 4128776 | tf_op jit(solution)/shard_map/cond/branch_1_fun/ppermute | solution.py:377
  443.9 56.0 %collective-permute-start.50 = (bf16[3,4,1,32,1792]{4,3,2,1,0:T(8,128)(2,1)}, bf16[3,4,1,32,1792]{4,3,2,1,0:T(8,128)(2,1)S(1)}, u32[]{:S(2)}, u32[]{:S(2)}) collective-permute-start(bf16[3,4,1,32,1792]{4,3,2,1,0:T(8,128)(2,1)} %pack.91), channel_id=1, source_target_pairs={{0,2},{2,0},{4,6},{6,4},{1,3},{3,1},{5,7},{7,5},{8,10},{10,8},{12,... | collective-permute-start | bytes 4128776 | tf_op jit(solution)/shard_map/cond/branch_1_fun/ppermute | solution.py:377
  468.6 56.2 %collective-permute-start.61 = (bf16[3,4,1,32,1792]{4,3,2,1,0:T(8,128)(2,1)}, bf16[3,4,1,32,1792]{4,3,2,1,0:T(8,128)(2,1)}, u32[]{:S(2)}, u32[]{:S(2)}) collective-permute-start(bf16[3,4,1,32,1792]{4,3,2,1,0:T(8,128)(2,1)} %pack.101), channel_id=1, source_target_pairs={{2,4},{4,2},{0,1},{6,7},{3,5},{5,3},{1,0},{7,6},{10,12},{12,10},{8... | collective-permute-start | bytes 4128776 | tf_op jit(solution)/shard_map/cond/branch_1_fun/ppermute | solution.py:386
  497.2 57.2 %collective-permute-start.58 = (bf16[3,4,1,32,1792]{4,3,2,1,0:T(8,128)(2,1)}, bf16[3,4,1,32,1792]{4,3,2,1,0:T(8,128)(2,1)}, u32[]{:S(2)}, u32[]{:S(2)}) collective-permute-start(bf16[3,4,1,32,1792]{4,3,2,1,0:T(8,128)(2,1)} %pack.98), channel_id=1, source_target_pairs={{2,4},{4,2},{0,1},{6,7},{3,5},{5,3},{1,0},{7,6},{10,12},{12,10},{8... | collective-permute-start | bytes 4128776 | tf_op jit(solution)/shard_map/cond/branch_1_fun/ppermute | solution.py:386
  505.6 79.4 %collective-permute-start.45 = (bf16[4,4,1,32,1792]{4,3,2,1,0:T(8,128)(2,1)}, bf16[4,4,1,32,1792]{4,3,2,1,0:T(8,128)(2,1)}, u32[]{:S(2)}, u32[]{:S(2)}) collective-permute-start(bf16[4,4,1,32,1792]{4,3,2,1,0:T(8,128)(2,1)} %pack.88), channel_id=1, source_target_pairs={{0,1},{2,3},{4,5},{6,7},{1,0},{3,2},{5,4},{7,6},{8,9},{10,11},{12,... | collective-permute-start | bytes 5505032 | tf_op jit(solution)/shard_map/cond/branch_1_fun/ppermute | solution.py:333
  (74 other events, 927.2 us)
Sparse Core Ops, SparseCore 0:
  10.2 28.9 all-gather.1
  166.6 97.2 all-reduce.5
  288.4 78.1 reduce-scatter.4
